TPU v7x, 256 devices: a whole 4x4x8 slice. The times are simulated.
256 devices in a mesh: down: 64 (over x, z_hi, y), cross: 4 (over z_lo, core).
Axes of the slice: x: 4, y: 4, z: 8 (z_hi: 4, z_lo: 2; z = z_hi * 2 + z_lo), core: 2. Of those that a mesh axis runs over, the one named last changes fastest.
Arguments:
- fields: float32 [4, 512, 256, 128], P(None, 'down', 'cross'), may hold values from -4 to 4
- embers: float32 [7, 64, 4, 6, 256], P(None, 'down', 'cross'), may hold values from 0.05 to 1
- counts: int32 [64, 4, 6], P('down', 'cross'), may hold values from 0 to 256, as said below
Outputs:
- advanced: float32 [4, 512, 256, 128], P(None, 'down', 'cross')
- landed: float32 [4, 64, 4, 6, 256], P(None, 'down', 'cross')
Inputs may be any that keep to these rules, and one draw needn't show every extreme that they name: `counts`: live records fill the leading slots of a buffer; some buffer is full in every draw.
All inputs are finite; a program needn't handle non-finite values.
Results may differ from a plain program's by a relative error of at most 0.0003.
Values sent between devices are 32-bit elements; how exact they have to be, the bound alone decides.
No kernel may reach another device: no remote copies, remote signals or barrier semaphores. Data moves between devices by JAX's collectives and lax.ppermute only.
A program may use at most 64 MiB of HBM per device.

v0:
```python
import jax
import jax.numpy as jnp
from jax import lax
from jax.sharding import PartitionSpec as P

STEPS = 6


HORIZONTAL_MIX = 0.1
VERTICAL_MIX = 0.1
ADVECTION = 0.25
DRAG_RATE = 0.6
BURN_RATE = 0.5
HEAT_YIELD = 4.0
DESTINATIONS = ((1, -1), (1, 0), (1, 1), (2, -1), (2, 0), (2, 1))


def shifted_2(x, axis, by):
    size = lax.axis_size(axis)
    pairs = [(i, i + by) for i in range(size) if 0 <= i + by < size]
    return lax.ppermute(x, axis, pairs)


def with_halo(x, sides, width):
    for axis, dim in sides:
        size, length = (lax.axis_size(axis), x.shape[dim])
        up = [(i, (i + 1) % size) for i in range(size - 1)]
        down = [(j, i) for i, j in up]
        last = lax.slice_in_dim(x, length - width, length, axis=dim)
        leading = lax.slice_in_dim(x, 0, width, axis=dim)
        before = lax.ppermute(last, axis, up)
        after = lax.ppermute(leading, axis, down)
        x = jnp.concatenate([before, x, after], axis=dim)
    return x


def advance(padded):
    centre = padded[:, 1:-1, 1:-1]
    eastern = padded[:, 2:, 1:-1]
    western = padded[:, :-2, 1:-1]
    northern = padded[:, 1:-1, 2:]
    southern = padded[:, 1:-1, :-2]
    upper_level = jnp.concatenate([centre[..., 1:], centre[..., -1:]], axis=-1)
    lower_level = jnp.concatenate([centre[..., :1], centre[..., :-1]], axis=-1)
    spread = eastern + western + northern + southern - 4.0 * centre
    column_mix = upper_level + lower_level - 2.0 * centre
    carried = centre[0:1] * (eastern - western) * 0.5 + centre[1:2] * (northern - southern) * 0.5
    return centre + HORIZONTAL_MIX * spread + VERTICAL_MIX * column_mix - ADVECTION * carried


def tent_weights(position, cell_count):
    centres = jnp.arange(cell_count).astype(jnp.float32) + 0.5
    return jnp.maximum(0.0, 1.0 - jnp.abs(position[:, None] - centres[None, :]))


def ember_update(tile_fields, records):
    cells_down = tile_fields.shape[1]
    cells_cross = tile_fields.shape[2]
    levels = tile_fields.shape[3]
    weight_down = tent_weights(records[0] * cells_down, cells_down)
    weight_cross = tent_weights(records[1] * cells_cross, cells_cross)
    weight_level = tent_weights(records[2] * levels, levels)
    column = jnp.einsum("kxyz,ez->kxye", tile_fields, weight_level, precision=lax.Precision.HIGHEST)
    across = jnp.sum(column * weight_cross.T[None, None], axis=2)
    sampled = jnp.sum(across * weight_down.T[None], axis=1)
    ember_mass = records[5]
    burned = ember_mass * BURN_RATE * jax.nn.sigmoid(records[6] + sampled[2] - sampled[3])
    living = (ember_mass > 0.0).astype(jnp.float32)
    landed = (
        jnp.stack(
            [
                records[3] + DRAG_RATE * (sampled[0] - records[3]),
                records[4] + DRAG_RATE * (sampled[1] - records[4]),
                records[6] + DRAG_RATE * (sampled[2] - records[6]),
                ember_mass - burned,
            ]
        )
        * living[None]
    )
    spread = (
        weight_down[:, :, None] * weight_cross[:, None, :] * (HEAT_YIELD * burned)[:, None, None]
    )
    spread = spread.reshape(records.shape[1], cells_down * cells_cross)
    deposit = jnp.dot(spread.T, weight_level, precision=lax.Precision.HIGHEST)
    return (landed, deposit.reshape(cells_down, cells_cross, levels))


def local(fields, embers, counts):
    slot_count = embers.shape[3]
    capacity = embers.shape[4]
    slot_index = jnp.arange(capacity)
    live_mask = (slot_index[None, :] < counts[0, 0][:, None]).astype(jnp.float32)
    outgoing = embers[:, 0, 0] * live_mask[None]
    arrived = []
    for target in range(slot_count):
        down_step, cross_step = DESTINATIONS[target]
        shifted = shifted_2(outgoing[:, target], "down", down_step)
        if cross_step != 0:
            shifted = shifted_2(shifted, "cross", cross_step)
        arrived.append(shifted)
    block_rows = 256
    deposit = jnp.zeros(fields.shape[1:], jnp.float32)
    results = []
    for target in range(slot_count):
        records = arrived[target]
        live_count = jnp.sum((records[5] > 0.0).astype(jnp.int32))
        passes = (live_count + block_rows - 1) // block_rows

        def one_pass(iteration, loop_state, records=records):
            finished, heat_sum = loop_state
            updated, extra_heat = ember_update(fields, records)
            return (updated, heat_sum + extra_heat)

        finished, deposit = lax.fori_loop(
            0, passes, one_pass, (jnp.zeros((4, capacity), jnp.float32), deposit)
        )
        results.append(finished)
    landed = jnp.stack(results, axis=1)[:, None, None]
    current = fields
    for step_index in range(STEPS):
        padded = with_halo(current, (("down", 1), ("cross", 2)), 1)
        current = advance(padded)
    advanced = jnp.concatenate([current[:2], current[2:3] + deposit[None], current[3:]], axis=0)
    return (advanced, landed)


def solution(mesh):
    placed = (
        P(None, "down", "cross", None),
        P(None, "down", "cross", None, None),
        P("down", "cross", None),
    )
    return jax.shard_map(
        local,
        mesh=mesh,
        in_specs=placed,
        out_specs=(P(None, "down", "cross", None), P(None, "down", "cross", None, None)),
        check_vma=False,
    )
```

profile of v0, /device:TPU:7, one launch (start us, length us, event | category | flops | bytes accessed | tf_op | source)
XLA Modules:
  0.0 246.2 jit_solution(8158394117328595635)
XLA Ops:
  2.3 3.2 %collective-permute-start.1 = (f32[4,1,64,128]{3,2,1,0:T(8,128)}, f32[4,1,64,128]{3,2,1,0:T(8,128)S(1)}, u32[]{:S(2)}, u32[]{:S(2)}) collective-permute-start(f32[4,1,64,128]{3,2,1,0:T(8,128)} %get-tuple-element.1101), channel_id=1, source_target_pairs={{0,4},{4,8},{8,12},{12,16},{16,20},{20,24},{24,28},{28,32},{32,36}... | collective-permute-start | bytes 393224 | tf_op jit(solution)/shard_map/ppermute | solution.py:31
  7.1 3.2 %collective-permute-start.24 = (f32[7,256]{1,0:T(8,128)S(1)}, f32[7,256]{1,0:T(8,128)S(1)}, u32[]{:S(2)}, u32[]{:S(2)}) collective-permute-start(f32[7,256]{1,0:T(8,128)S(1)} %get-tuple-element.1111), channel_id=1, source_target_pairs={{0,4},{4,8},{8,12},{12,16},{16,20},{20,24},{24,28},{28,32},{32,36}... | collective-permute-start | bytes 21512 | tf_op jit(solution)/shard_map/ppermute | solution.py:21
  10.3 5.9 %collective-permute-start.32 = (f32[7,256]{1,0:T(8,128)S(1)}, f32[7,256]{1,0:T(8,128)S(1)}, u32[]{:S(2)}, u32[]{:S(2)}) collective-permute-start(f32[7,256]{1,0:T(8,128)S(1)} %get-tuple-element.1106), channel_id=1, source_target_pairs={{0,8},{4,12},{8,16},{12,20},{16,24},{20,28},{24,32},{28,36},{32,40... | collective-permute-start | bytes 21512 | tf_op jit(solution)/shard_map/ppermute | solution.py:21
  16.2 2.6 %collective-permute-start.26 = (f32[7,256]{1,0:T(8,128)S(1)}, f32[7,256]{1,0:T(8,128)S(1)}, u32[]{:S(2)}, u32[]{:S(2)}) collective-permute-start(f32[7,256]{1,0:T(8,128)S(1)} %get-tuple-element.1110), channel_id=1, source_target_pairs={{0,4},{4,8},{8,12},{12,16},{16,20},{20,24},{24,28},{28,32},{32,36}... | collective-permute-start | bytes 21512 | tf_op jit(solution)/shard_map/ppermute | solution.py:21
  18.8 2.7 %collective-permute-start.27 = (f32[7,256]{1,0:T(8,128)S(1)}, f32[7,256]{1,0:T(8,128)S(1)}, u32[]{:S(2)}, u32[]{:S(2)}) collective-permute-start(f32[7,256]{1,0:T(8,128)S(1)} %get-tuple-element.1109), channel_id=1, source_target_pairs={{0,4},{4,8},{8,12},{12,16},{16,20},{20,24},{24,28},{28,32},{32,36}... | collective-permute-start | bytes 21512 | tf_op jit(solution)/shard_map/ppermute | solution.py:21
  21.5 2.9 %fusion.174 = (f32[4,8,64,1]{3,2,1,0:T(8,128)S(1)}, f32[4,8,64,1]{3,2,1,0:T(8,128)}) fusion(f32[4,8,64,128]{3,2,1,0:T(8,128)} %param.15), kind=kLoop, calls=%fused_computation.411 | loop fusion | bytes 32768 | tf_op jit(solution)/shard_map/slice | solution.py:44
  26.9 8.3 %collective-permute-start.31 = (f32[7,256]{1,0:T(8,128)S(1)}, f32[7,256]{1,0:T(8,128)S(1)}, u32[]{:S(2)}, u32[]{:S(2)}) collective-permute-start(f32[7,256]{1,0:T(8,128)S(1)} %get-tuple-element.1107), channel_id=1, source_target_pairs={{0,8},{4,12},{8,16},{12,20},{16,24},{20,28},{24,32},{28,36},{32,40... | collective-permute-start | bytes 21512 | tf_op jit(solution)/shard_map/ppermute | solution.py:21
  38.3 5.2 %collective-permute-start.33 = (f32[7,256]{1,0:T(8,128)S(1)}, f32[7,256]{1,0:T(8,128)S(1)}, u32[]{:S(2)}, u32[]{:S(2)}) collective-permute-start(f32[7,256]{1,0:T(8,128)S(1)} %collective-permute-done.32), channel_id=1, source_target_pairs={{0,1},{1,2},{2,3},{4,5},{5,6},{6,7},{8,9},{9,10},{10,11},{12,13},{... | collective-permute-start | bytes 21512 | tf_op jit(solution)/shard_map/ppermute | solution.py:21
  46.0 7.8 %collective-permute-start = (f32[4,1,64,128]{3,2,1,0:T(8,128)}, f32[4,1,64,128]{3,2,1,0:T(8,128)}, u32[]{:S(2)}, u32[]{:S(2)}) collective-permute-start(f32[4,1,64,128]{3,2,1,0:T(8,128)} %get-tuple-element.1100), channel_id=1, source_target_pairs={{4,0},{8,4},{12,8},{16,12},{20,16},{24,20},{28,24},{32,28},{36,32}... | collective-permute-start | bytes 393224 | tf_op jit(solution)/shard_map/ppermute | solution.py:32
  55.8 3.6 %collective-permute-start.28 = (f32[7,256]{1,0:T(8,128)S(1)}, f32[7,256]{1,0:T(8,128)S(1)}, u32[]{:S(2)}, u32[]{:S(2)}) collective-permute-start(f32[7,256]{1,0:T(8,128)S(1)} %collective-permute-done.27), channel_id=1, source_target_pairs={{0,1},{1,2},{2,3},{4,5},{5,6},{6,7},{8,9},{9,10},{10,11},{12,13},{... | collective-permute-start | bytes 21512 | tf_op jit(solution)/shard_map/ppermute | solution.py:21
  110.2 3.1 %collective-permute-start.3 = (f32[4,10,1,128]{3,2,1,0:T(1,128)S(1)}, f32[4,10,1,128]{3,2,1,0:T(1,128)S(1)}, u32[]{:S(2)}, u32[]{:S(2)}) collective-permute-start(f32[4,10,1,128]{3,2,1,0:T(1,128)S(1)} %get-tuple-element.1055), channel_id=1, source_target_pairs={{0,1},{1,2},{2,3},{4,5},{5,6},{6,7},{8,9},{9,10},{10,11},{12,13},{... | collective-permute-start | bytes 61448 | tf_op jit(solution)/shard_map/ppermute | solution.py:31
  121.2 2.7 %collective-permute-start.4 = (f32[4,1,64,128]{3,2,1,0:T(8,128)S(1)}, f32[4,1,64,128]{3,2,1,0:T(8,128)S(1)}, u32[]{:S(2)}, u32[]{:S(2)}) collective-permute-start(f32[4,1,64,128]{3,2,1,0:T(8,128)S(1)} %get-tuple-element.1093), channel_id=1, source_target_pairs={{4,0},{8,4},{12,8},{16,12},{20,16},{24,20},{28,24},{32,28},{36,32}... | collective-permute-start | bytes 393224 | tf_op jit(solution)/shard_map/ppermute | solution.py:32
  123.8 2.6 %collective-permute-start.5 = (f32[4,1,64,128]{3,2,1,0:T(8,128)S(1)}, f32[4,1,64,128]{3,2,1,0:T(8,128)S(1)}, u32[]{:S(2)}, u32[]{:S(2)}) collective-permute-start(f32[4,1,64,128]{3,2,1,0:T(8,128)S(1)} %get-tuple-element.1092), channel_id=1, source_target_pairs={{0,4},{4,8},{8,12},{12,16},{16,20},{20,24},{24,28},{28,32},{32,36}... | collective-permute-start | bytes 393224 | tf_op jit(solution)/shard_map/ppermute | solution.py:31
  128.1 7.1 %collective-permute-done.5 = f32[4,1,64,128]{3,2,1,0:T(8,128)S(1)} collective-permute-done((f32[4,1,64,128]{3,2,1,0:T(8,128)S(1)}, f32[4,1,64,128]{3,2,1,0:T(8,128)S(1)}, u32[]{:S(2)}, u32[]{:S(2)}) %collective-permute-start.5) | collective-permute-done | bytes 131104 | tf_op jit(solution)/shard_map/ppermute | solution.py:31
  135.2 4.9 %collective-permute-start.7 = (f32[4,10,1,128]{3,2,1,0:T(1,128)S(1)}, f32[4,10,1,128]{3,2,1,0:T(1,128)S(1)}, u32[]{:S(2)}, u32[]{:S(2)}) collective-permute-start(f32[4,10,1,128]{3,2,1,0:T(1,128)S(1)} %get-tuple-element.1053), channel_id=1, source_target_pairs={{0,1},{1,2},{2,3},{4,5},{5,6},{6,7},{8,9},{9,10},{10,11},{12,13},{... | collective-permute-start | bytes 61448 | tf_op jit(solution)/shard_map/ppermute | solution.py:31
  142.0 3.1 %collective-permute-done.6 = f32[4,10,1,128]{3,2,1,0:T(1,128)S(1)} collective-permute-done((f32[4,10,1,128]{3,2,1,0:T(1,128)S(1)}, f32[4,10,1,128]{3,2,1,0:T(1,128)S(1)}, u32[]{:S(2)}, u32[]{:S(2)}) %collective-permute-start.6) | collective-permute-done | bytes 20512 | tf_op jit(solution)/shard_map/ppermute | solution.py:32
  148.9 3.4 %collective-permute-start.9 = (f32[4,1,64,128]{3,2,1,0:T(8,128)S(1)}, f32[4,1,64,128]{3,2,1,0:T(8,128)S(1)}, u32[]{:S(2)}, u32[]{:S(2)}) collective-permute-start(f32[4,1,64,128]{3,2,1,0:T(8,128)S(1)} %get-tuple-element.1084), channel_id=1, source_target_pairs={{0,4},{4,8},{8,12},{12,16},{16,20},{20,24},{24,28},{28,32},{32,36}... | collective-permute-start | bytes 393224 | tf_op jit(solution)/shard_map/ppermute | solution.py:31
  153.1 6.6 %collective-permute-done.9 = f32[4,1,64,128]{3,2,1,0:T(8,128)S(1)} collective-permute-done((f32[4,1,64,128]{3,2,1,0:T(8,128)S(1)}, f32[4,1,64,128]{3,2,1,0:T(8,128)S(1)}, u32[]{:S(2)}, u32[]{:S(2)}) %collective-permute-start.9) | collective-permute-done | bytes 131104 | tf_op jit(solution)/shard_map/ppermute | solution.py:31
  159.7 4.9 %collective-permute-start.11 = (f32[4,10,1,128]{3,2,1,0:T(1,128)S(1)}, f32[4,10,1,128]{3,2,1,0:T(1,128)S(1)}, u32[]{:S(2)}, u32[]{:S(2)}) collective-permute-start(f32[4,10,1,128]{3,2,1,0:T(1,128)S(1)} %get-tuple-element.1051), channel_id=1, source_target_pairs={{0,1},{1,2},{2,3},{4,5},{5,6},{6,7},{8,9},{9,10},{10,11},{12,13},{... | collective-permute-start | bytes 61448 | tf_op jit(solution)/shard_map/ppermute | solution.py:31
  166.6 3.1 %collective-permute-done.10 = f32[4,10,1,128]{3,2,1,0:T(1,128)S(1)} collective-permute-done((f32[4,10,1,128]{3,2,1,0:T(1,128)S(1)}, f32[4,10,1,128]{3,2,1,0:T(1,128)S(1)}, u32[]{:S(2)}, u32[]{:S(2)}) %collective-permute-start.10) | collective-permute-done | bytes 20512 | tf_op jit(solution)/shard_map/ppermute | solution.py:32
  173.5 3.4 %collective-permute-start.13 = (f32[4,1,64,128]{3,2,1,0:T(8,128)S(1)}, f32[4,1,64,128]{3,2,1,0:T(8,128)S(1)}, u32[]{:S(2)}, u32[]{:S(2)}) collective-permute-start(f32[4,1,64,128]{3,2,1,0:T(8,128)S(1)} %get-tuple-element.1076), channel_id=1, source_target_pairs={{0,4},{4,8},{8,12},{12,16},{16,20},{20,24},{24,28},{28,32},{32,36}... | collective-permute-start | bytes 393224 | tf_op jit(solution)/shard_map/ppermute | solution.py:31
  177.2 7.0 %collective-permute-done.13 = f32[4,1,64,128]{3,2,1,0:T(8,128)S(1)} collective-permute-done((f32[4,1,64,128]{3,2,1,0:T(8,128)S(1)}, f32[4,1,64,128]{3,2,1,0:T(8,128)S(1)}, u32[]{:S(2)}, u32[]{:S(2)}) %collective-permute-start.13) | collective-permute-done | bytes 131104 | tf_op jit(solution)/shard_map/ppermute | solution.py:31
  184.3 4.9 %collective-permute-start.15 = (f32[4,10,1,128]{3,2,1,0:T(1,128)S(1)}, f32[4,10,1,128]{3,2,1,0:T(1,128)S(1)}, u32[]{:S(2)}, u32[]{:S(2)}) collective-permute-start(f32[4,10,1,128]{3,2,1,0:T(1,128)S(1)} %get-tuple-element.1049), channel_id=1, source_target_pairs={{0,1},{1,2},{2,3},{4,5},{5,6},{6,7},{8,9},{9,10},{10,11},{12,13},{... | collective-permute-start | bytes 61448 | tf_op jit(solution)/shard_map/ppermute | solution.py:31
  191.2 3.9 %collective-permute-done.14 = f32[4,10,1,128]{3,2,1,0:T(1,128)S(1)} collective-permute-done((f32[4,10,1,128]{3,2,1,0:T(1,128)S(1)}, f32[4,10,1,128]{3,2,1,0:T(1,128)S(1)}, u32[]{:S(2)}, u32[]{:S(2)}) %collective-permute-start.14) | collective-permute-done | bytes 20512 | tf_op jit(solution)/shard_map/ppermute | solution.py:32
  198.9 3.4 %collective-permute-start.17 = (f32[4,1,64,128]{3,2,1,0:T(8,128)S(1)}, f32[4,1,64,128]{3,2,1,0:T(8,128)S(1)}, u32[]{:S(2)}, u32[]{:S(2)}) collective-permute-start(f32[4,1,64,128]{3,2,1,0:T(8,128)S(1)} %get-tuple-element.1068), channel_id=1, source_target_pairs={{0,4},{4,8},{8,12},{12,16},{16,20},{20,24},{24,28},{28,32},{32,36}... | collective-permute-start | bytes 393224 | tf_op jit(solution)/shard_map/ppermute | solution.py:31
  202.6 7.0 %collective-permute-done.17 = f32[4,1,64,128]{3,2,1,0:T(8,128)S(1)} collective-permute-done((f32[4,1,64,128]{3,2,1,0:T(8,128)S(1)}, f32[4,1,64,128]{3,2,1,0:T(8,128)S(1)}, u32[]{:S(2)}, u32[]{:S(2)}) %collective-permute-start.17) | collective-permute-done | bytes 131104 | tf_op jit(solution)/shard_map/ppermute | solution.py:31
  209.7 4.1 %collective-permute-start.19 = (f32[4,10,1,128]{3,2,1,0:T(1,128)S(1)}, f32[4,10,1,128]{3,2,1,0:T(1,128)S(1)}, u32[]{:S(2)}, u32[]{:S(2)}) collective-permute-start(f32[4,10,1,128]{3,2,1,0:T(1,128)S(1)} %get-tuple-element.1047), channel_id=1, source_target_pairs={{0,1},{1,2},{2,3},{4,5},{5,6},{6,7},{8,9},{9,10},{10,11},{12,13},{... | collective-permute-start | bytes 61448 | tf_op jit(solution)/shard_map/ppermute | solution.py:31
  215.9 3.1 %collective-permute-done.18 = f32[4,10,1,128]{3,2,1,0:T(1,128)S(1)} collective-permute-done((f32[4,10,1,128]{3,2,1,0:T(1,128)S(1)}, f32[4,10,1,128]{3,2,1,0:T(1,128)S(1)}, u32[]{:S(2)}, u32[]{:S(2)}) %collective-permute-start.18) | collective-permute-done | bytes 20512 | tf_op jit(solution)/shard_map/ppermute | solution.py:32
  222.7 3.4 %collective-permute-start.21 = (f32[4,1,64,128]{3,2,1,0:T(8,128)S(1)}, f32[4,1,64,128]{3,2,1,0:T(8,128)S(1)}, u32[]{:S(2)}, u32[]{:S(2)}) collective-permute-start(f32[4,1,64,128]{3,2,1,0:T(8,128)S(1)} %get-tuple-element.1060), channel_id=1, source_target_pairs={{0,4},{4,8},{8,12},{12,16},{16,20},{20,24},{24,28},{28,32},{32,36}... | collective-permute-start | bytes 393224 | tf_op jit(solution)/shard_map/ppermute | solution.py:31
  226.5 7.0 %collective-permute-done.21 = f32[4,1,64,128]{3,2,1,0:T(8,128)S(1)} collective-permute-done((f32[4,1,64,128]{3,2,1,0:T(8,128)S(1)}, f32[4,1,64,128]{3,2,1,0:T(8,128)S(1)}, u32[]{:S(2)}, u32[]{:S(2)}) %collective-permute-start.21) | collective-permute-done | bytes 131104 | tf_op jit(solution)/shard_map/ppermute | solution.py:31
  233.6 4.9 %collective-permute-start.23 = (f32[4,10,1,128]{3,2,1,0:T(1,128)S(1)}, f32[4,10,1,128]{3,2,1,0:T(1,128)S(1)}, u32[]{:S(2)}, u32[]{:S(2)}) collective-permute-start(f32[4,10,1,128]{3,2,1,0:T(1,128)S(1)} %get-tuple-element.1045), channel_id=1, source_target_pairs={{0,1},{1,2},{2,3},{4,5},{5,6},{6,7},{8,9},{9,10},{10,11},{12,13},{... | collective-permute-start | bytes 61448 | tf_op jit(solution)/shard_map/ppermute | solution.py:31
  240.5 3.1 %collective-permute-done.22 = f32[4,10,1,128]{3,2,1,0:T(1,128)S(1)} collective-permute-done((f32[4,10,1,128]{3,2,1,0:T(1,128)S(1)}, f32[4,10,1,128]{3,2,1,0:T(1,128)S(1)}, u32[]{:S(2)}, u32[]{:S(2)}) %collective-permute-start.22) | collective-permute-done | bytes 20512 | tf_op jit(solution)/shard_map/ppermute | solution.py:32
  (272 shorter events, 105.8 us)
Async XLA Ops:
  2.3 106.6 %collective-permute-start.1 = (f32[4,1,64,128]{3,2,1,0:T(8,128)}, f32[4,1,64,128]{3,2,1,0:T(8,128)S(1)}, u32[]{:S(2)}, u32[]{:S(2)}) collective-permute-start(f32[4,1,64,128]{3,2,1,0:T(8,128)} %get-tuple-element.1101), channel_id=1, source_target_pairs={{0,4},{4,8},{8,12},{12,16},{16,20},{20,24},{24,28},{28,32},{32,36}... | collective-permute-start | bytes 393224 | tf_op jit(solution)/shard_map/ppermute | solution.py:31
  7.1 39.0 %collective-permute-start.24 = (f32[7,256]{1,0:T(8,128)S(1)}, f32[7,256]{1,0:T(8,128)S(1)}, u32[]{:S(2)}, u32[]{:S(2)}) collective-permute-start(f32[7,256]{1,0:T(8,128)S(1)} %get-tuple-element.1111), channel_id=1, source_target_pairs={{0,4},{4,8},{8,12},{12,16},{16,20},{20,24},{24,28},{28,32},{32,36}... | collective-permute-start | bytes 21512 | tf_op jit(solution)/shard_map/ppermute | solution.py:21
  10.3 25.6 %collective-permute-start.32 = (f32[7,256]{1,0:T(8,128)S(1)}, f32[7,256]{1,0:T(8,128)S(1)}, u32[]{:S(2)}, u32[]{:S(2)}) collective-permute-start(f32[7,256]{1,0:T(8,128)S(1)} %get-tuple-element.1106), channel_id=1, source_target_pairs={{0,8},{4,12},{8,16},{12,20},{16,24},{20,28},{24,32},{28,36},{32,40... | collective-permute-start | bytes 21512 | tf_op jit(solution)/shard_map/ppermute | solution.py:21
  16.2 10.7 %collective-permute-start.26 = (f32[7,256]{1,0:T(8,128)S(1)}, f32[7,256]{1,0:T(8,128)S(1)}, u32[]{:S(2)}, u32[]{:S(2)}) collective-permute-start(f32[7,256]{1,0:T(8,128)S(1)} %get-tuple-element.1110), channel_id=1, source_target_pairs={{0,4},{4,8},{8,12},{12,16},{16,20},{20,24},{24,28},{28,32},{32,36}... | collective-permute-start | bytes 21512 | tf_op jit(solution)/shard_map/ppermute | solution.py:21
  18.8 35.1 %collective-permute-start.27 = (f32[7,256]{1,0:T(8,128)S(1)}, f32[7,256]{1,0:T(8,128)S(1)}, u32[]{:S(2)}, u32[]{:S(2)}) collective-permute-start(f32[7,256]{1,0:T(8,128)S(1)} %get-tuple-element.1109), channel_id=1, source_target_pairs={{0,4},{4,8},{8,12},{12,16},{16,20},{20,24},{24,28},{28,32},{32,36}... | collective-permute-start | bytes 21512 | tf_op jit(solution)/shard_map/ppermute | solution.py:21
  26.9 11.4 %collective-permute-start.31 = (f32[7,256]{1,0:T(8,128)S(1)}, f32[7,256]{1,0:T(8,128)S(1)}, u32[]{:S(2)}, u32[]{:S(2)}) collective-permute-start(f32[7,256]{1,0:T(8,128)S(1)} %get-tuple-element.1107), channel_id=1, source_target_pairs={{0,8},{4,12},{8,16},{12,20},{16,24},{20,28},{24,32},{28,36},{32,40... | collective-permute-start | bytes 21512 | tf_op jit(solution)/shard_map/ppermute | solution.py:21
  35.8 20.0 %collective-permute-start.29 = (f32[7,256]{1,0:T(8,128)S(1)}, f32[7,256]{1,0:T(8,128)S(1)}, u32[]{:S(2)}, u32[]{:S(2)}) collective-permute-start(f32[7,256]{1,0:T(8,128)S(1)} %get-tuple-element.1108), channel_id=1, source_target_pairs={{0,8},{4,12},{8,16},{12,20},{16,24},{20,28},{24,32},{28,36},{32,40... | collective-permute-start | bytes 21512 | tf_op jit(solution)/shard_map/ppermute | solution.py:21
  38.3 21.2 %collective-permute-start.33 = (f32[7,256]{1,0:T(8,128)S(1)}, f32[7,256]{1,0:T(8,128)S(1)}, u32[]{:S(2)}, u32[]{:S(2)}) collective-permute-start(f32[7,256]{1,0:T(8,128)S(1)} %collective-permute-done.32), channel_id=1, source_target_pairs={{0,1},{1,2},{2,3},{4,5},{5,6},{6,7},{8,9},{9,10},{10,11},{12,13},{... | collective-permute-start | bytes 21512 | tf_op jit(solution)/shard_map/ppermute | solution.py:21
  46.0 63.0 %collective-permute-start = (f32[4,1,64,128]{3,2,1,0:T(8,128)}, f32[4,1,64,128]{3,2,1,0:T(8,128)}, u32[]{:S(2)}, u32[]{:S(2)}) collective-permute-start(f32[4,1,64,128]{3,2,1,0:T(8,128)} %get-tuple-element.1100), channel_id=1, source_target_pairs={{4,0},{8,4},{12,8},{16,12},{20,16},{24,20},{28,24},{32,28},{36,32}... | collective-permute-start | bytes 393224 | tf_op jit(solution)/shard_map/ppermute | solution.py:32
  53.9 8.7 %collective-permute-start.25 = (f32[7,256]{1,0:T(8,128)S(1)}, f32[7,256]{1,0:T(8,128)S(1)}, u32[]{:S(2)}, u32[]{:S(2)}) collective-permute-start(f32[7,256]{1,0:T(8,128)S(1)} %collective-permute-done.24), channel_id=1, source_target_pairs={{1,0},{2,1},{3,2},{5,4},{6,5},{7,6},{9,8},{10,9},{11,10},{13,12},{... | collective-permute-start | bytes 21512 | tf_op jit(solution)/shard_map/ppermute | solution.py:21
  55.8 6.1 %collective-permute-start.28 = (f32[7,256]{1,0:T(8,128)S(1)}, f32[7,256]{1,0:T(8,128)S(1)}, u32[]{:S(2)}, u32[]{:S(2)}) collective-permute-start(f32[7,256]{1,0:T(8,128)S(1)} %collective-permute-done.27), channel_id=1, source_target_pairs={{0,1},{1,2},{2,3},{4,5},{5,6},{6,7},{8,9},{9,10},{10,11},{12,13},{... | collective-permute-start | bytes 21512 | tf_op jit(solution)/shard_map/ppermute | solution.py:21
  110.2 5.9 %collective-permute-start.3 = (f32[4,10,1,128]{3,2,1,0:T(1,128)S(1)}, f32[4,10,1,128]{3,2,1,0:T(1,128)S(1)}, u32[]{:S(2)}, u32[]{:S(2)}) collective-permute-start(f32[4,10,1,128]{3,2,1,0:T(1,128)S(1)} %get-tuple-element.1055), channel_id=1, source_target_pairs={{0,1},{1,2},{2,3},{4,5},{5,6},{6,7},{8,9},{9,10},{10,11},{12,13},{... | collective-permute-start | bytes 61448 | tf_op jit(solution)/shard_map/ppermute | solution.py:31
  113.3 5.1 %collective-permute-start.2 = (f32[4,10,1,128]{3,2,1,0:T(1,128)S(1)}, f32[4,10,1,128]{3,2,1,0:T(1,128)S(1)}, u32[]{:S(2)}, u32[]{:S(2)}) collective-permute-start(f32[4,10,1,128]{3,2,1,0:T(1,128)S(1)} %get-tuple-element.1054), channel_id=1, source_target_pairs={{1,0},{2,1},{3,2},{5,4},{6,5},{7,6},{9,8},{10,9},{11,10},{13,12},{... | collective-permute-start | bytes 61448 | tf_op jit(solution)/shard_map/ppermute | solution.py:32
  121.2 6.9 %collective-permute-start.4 = (f32[4,1,64,128]{3,2,1,0:T(8,128)S(1)}, f32[4,1,64,128]{3,2,1,0:T(8,128)S(1)}, u32[]{:S(2)}, u32[]{:S(2)}) collective-permute-start(f32[4,1,64,128]{3,2,1,0:T(8,128)S(1)} %get-tuple-element.1093), channel_id=1, source_target_pairs={{4,0},{8,4},{12,8},{16,12},{20,16},{24,20},{28,24},{32,28},{36,32}... | collective-permute-start | bytes 393224 | tf_op jit(solution)/shard_map/ppermute | solution.py:32
  123.8 11.3 %collective-permute-start.5 = (f32[4,1,64,128]{3,2,1,0:T(8,128)S(1)}, f32[4,1,64,128]{3,2,1,0:T(8,128)S(1)}, u32[]{:S(2)}, u32[]{:S(2)}) collective-permute-start(f32[4,1,64,128]{3,2,1,0:T(8,128)S(1)} %get-tuple-element.1092), channel_id=1, source_target_pairs={{0,4},{4,8},{8,12},{12,16},{16,20},{20,24},{24,28},{28,32},{32,36}... | collective-permute-start | bytes 393224 | tf_op jit(solution)/shard_map/ppermute | solution.py:31
  135.2 6.8 %collective-permute-start.7 = (f32[4,10,1,128]{3,2,1,0:T(1,128)S(1)}, f32[4,10,1,128]{3,2,1,0:T(1,128)S(1)}, u32[]{:S(2)}, u32[]{:S(2)}) collective-permute-start(f32[4,10,1,128]{3,2,1,0:T(1,128)S(1)} %get-tuple-element.1053), channel_id=1, source_target_pairs={{0,1},{1,2},{2,3},{4,5},{5,6},{6,7},{8,9},{9,10},{10,11},{12,13},{... | collective-permute-start | bytes 61448 | tf_op jit(solution)/shard_map/ppermute | solution.py:31
  140.1 5.1 %collective-permute-start.6 = (f32[4,10,1,128]{3,2,1,0:T(1,128)S(1)}, f32[4,10,1,128]{3,2,1,0:T(1,128)S(1)}, u32[]{:S(2)}, u32[]{:S(2)}) collective-permute-start(f32[4,10,1,128]{3,2,1,0:T(1,128)S(1)} %get-tuple-element.1052), channel_id=1, source_target_pairs={{1,0},{2,1},{3,2},{5,4},{6,5},{7,6},{9,8},{10,9},{11,10},{13,12},{... | collective-permute-start | bytes 61448 | tf_op jit(solution)/shard_map/ppermute | solution.py:32
  146.9 6.1 %collective-permute-start.8 = (f32[4,1,64,128]{3,2,1,0:T(8,128)S(1)}, f32[4,1,64,128]{3,2,1,0:T(8,128)S(1)}, u32[]{:S(2)}, u32[]{:S(2)}) collective-permute-start(f32[4,1,64,128]{3,2,1,0:T(8,128)S(1)} %get-tuple-element.1085), channel_id=1, source_target_pairs={{4,0},{8,4},{12,8},{16,12},{20,16},{24,20},{28,24},{32,28},{36,32}... | collective-permute-start | bytes 393224 | tf_op jit(solution)/shard_map/ppermute | solution.py:32
  148.9 10.8 %collective-permute-start.9 = (f32[4,1,64,128]{3,2,1,0:T(8,128)S(1)}, f32[4,1,64,128]{3,2,1,0:T(8,128)S(1)}, u32[]{:S(2)}, u32[]{:S(2)}) collective-permute-start(f32[4,1,64,128]{3,2,1,0:T(8,128)S(1)} %get-tuple-element.1084), channel_id=1, source_target_pairs={{0,4},{4,8},{8,12},{12,16},{16,20},{20,24},{24,28},{28,32},{32,36}... | collective-permute-start | bytes 393224 | tf_op jit(solution)/shard_map/ppermute | solution.py:31
  159.7 6.9 %collective-permute-start.11 = (f32[4,10,1,128]{3,2,1,0:T(1,128)S(1)}, f32[4,10,1,128]{3,2,1,0:T(1,128)S(1)}, u32[]{:S(2)}, u32[]{:S(2)}) collective-permute-start(f32[4,10,1,128]{3,2,1,0:T(1,128)S(1)} %get-tuple-element.1051), channel_id=1, source_target_pairs={{0,1},{1,2},{2,3},{4,5},{5,6},{6,7},{8,9},{9,10},{10,11},{12,13},{... | collective-permute-start | bytes 61448 | tf_op jit(solution)/shard_map/ppermute | solution.py:31
  164.6 5.1 %collective-permute-start.10 = (f32[4,10,1,128]{3,2,1,0:T(1,128)S(1)}, f32[4,10,1,128]{3,2,1,0:T(1,128)S(1)}, u32[]{:S(2)}, u32[]{:S(2)}) collective-permute-start(f32[4,10,1,128]{3,2,1,0:T(1,128)S(1)} %get-tuple-element.1050), channel_id=1, source_target_pairs={{1,0},{2,1},{3,2},{5,4},{6,5},{7,6},{9,8},{10,9},{11,10},{13,12},{... | collective-permute-start | bytes 61448 | tf_op jit(solution)/shard_map/ppermute | solution.py:32
  171.5 5.7 %collective-permute-start.12 = (f32[4,1,64,128]{3,2,1,0:T(8,128)S(1)}, f32[4,1,64,128]{3,2,1,0:T(8,128)S(1)}, u32[]{:S(2)}, u32[]{:S(2)}) collective-permute-start(f32[4,1,64,128]{3,2,1,0:T(8,128)S(1)} %get-tuple-element.1077), channel_id=1, source_target_pairs={{4,0},{8,4},{12,8},{16,12},{20,16},{24,20},{28,24},{32,28},{36,32}... | collective-permute-start | bytes 393224 | tf_op jit(solution)/shard_map/ppermute | solution.py:32
  173.5 10.8 %collective-permute-start.13 = (f32[4,1,64,128]{3,2,1,0:T(8,128)S(1)}, f32[4,1,64,128]{3,2,1,0:T(8,128)S(1)}, u32[]{:S(2)}, u32[]{:S(2)}) collective-permute-start(f32[4,1,64,128]{3,2,1,0:T(8,128)S(1)} %get-tuple-element.1076), channel_id=1, source_target_pairs={{0,4},{4,8},{8,12},{12,16},{16,20},{20,24},{24,28},{28,32},{32,36}... | collective-permute-start | bytes 393224 | tf_op jit(solution)/shard_map/ppermute | solution.py:31
  184.3 6.9 %collective-permute-start.15 = (f32[4,10,1,128]{3,2,1,0:T(1,128)S(1)}, f32[4,10,1,128]{3,2,1,0:T(1,128)S(1)}, u32[]{:S(2)}, u32[]{:S(2)}) collective-permute-start(f32[4,10,1,128]{3,2,1,0:T(1,128)S(1)} %get-tuple-element.1049), channel_id=1, source_target_pairs={{0,1},{1,2},{2,3},{4,5},{5,6},{6,7},{8,9},{9,10},{10,11},{12,13},{... | collective-permute-start | bytes 61448 | tf_op jit(solution)/shard_map/ppermute | solution.py:31
  189.3 5.9 %collective-permute-start.14 = (f32[4,10,1,128]{3,2,1,0:T(1,128)S(1)}, f32[4,10,1,128]{3,2,1,0:T(1,128)S(1)}, u32[]{:S(2)}, u32[]{:S(2)}) collective-permute-start(f32[4,10,1,128]{3,2,1,0:T(1,128)S(1)} %get-tuple-element.1048), channel_id=1, source_target_pairs={{1,0},{2,1},{3,2},{5,4},{6,5},{7,6},{9,8},{10,9},{11,10},{13,12},{... | collective-permute-start | bytes 61448 | tf_op jit(solution)/shard_map/ppermute | solution.py:32
  196.9 5.7 %collective-permute-start.16 = (f32[4,1,64,128]{3,2,1,0:T(8,128)S(1)}, f32[4,1,64,128]{3,2,1,0:T(8,128)S(1)}, u32[]{:S(2)}, u32[]{:S(2)}) collective-permute-start(f32[4,1,64,128]{3,2,1,0:T(8,128)S(1)} %get-tuple-element.1069), channel_id=1, source_target_pairs={{4,0},{8,4},{12,8},{16,12},{20,16},{24,20},{28,24},{32,28},{36,32}... | collective-permute-start | bytes 393224 | tf_op jit(solution)/shard_map/ppermute | solution.py:32
  198.9 10.8 %collective-permute-start.17 = (f32[4,1,64,128]{3,2,1,0:T(8,128)S(1)}, f32[4,1,64,128]{3,2,1,0:T(8,128)S(1)}, u32[]{:S(2)}, u32[]{:S(2)}) collective-permute-start(f32[4,1,64,128]{3,2,1,0:T(8,128)S(1)} %get-tuple-element.1068), channel_id=1, source_target_pairs={{0,4},{4,8},{8,12},{12,16},{16,20},{20,24},{24,28},{28,32},{32,36}... | collective-permute-start | bytes 393224 | tf_op jit(solution)/shard_map/ppermute | solution.py:31
  209.7 6.1 %collective-permute-start.19 = (f32[4,10,1,128]{3,2,1,0:T(1,128)S(1)}, f32[4,10,1,128]{3,2,1,0:T(1,128)S(1)}, u32[]{:S(2)}, u32[]{:S(2)}) collective-permute-start(f32[4,10,1,128]{3,2,1,0:T(1,128)S(1)} %get-tuple-element.1047), channel_id=1, source_target_pairs={{0,1},{1,2},{2,3},{4,5},{5,6},{6,7},{8,9},{9,10},{10,11},{12,13},{... | collective-permute-start | bytes 61448 | tf_op jit(solution)/shard_map/ppermute | solution.py:31
  213.9 5.1 %collective-permute-start.18 = (f32[4,10,1,128]{3,2,1,0:T(1,128)S(1)}, f32[4,10,1,128]{3,2,1,0:T(1,128)S(1)}, u32[]{:S(2)}, u32[]{:S(2)}) collective-permute-start(f32[4,10,1,128]{3,2,1,0:T(1,128)S(1)} %get-tuple-element.1046), channel_id=1, source_target_pairs={{1,0},{2,1},{3,2},{5,4},{6,5},{7,6},{9,8},{10,9},{11,10},{13,12},{... | collective-permute-start | bytes 61448 | tf_op jit(solution)/shard_map/ppermute | solution.py:32
  220.8 5.7 %collective-permute-start.20 = (f32[4,1,64,128]{3,2,1,0:T(8,128)S(1)}, f32[4,1,64,128]{3,2,1,0:T(8,128)S(1)}, u32[]{:S(2)}, u32[]{:S(2)}) collective-permute-start(f32[4,1,64,128]{3,2,1,0:T(8,128)S(1)} %get-tuple-element.1061), channel_id=1, source_target_pairs={{4,0},{8,4},{12,8},{16,12},{20,16},{24,20},{28,24},{32,28},{36,32}... | collective-permute-start | bytes 393224 | tf_op jit(solution)/shard_map/ppermute | solution.py:32
  222.7 10.8 %collective-permute-start.21 = (f32[4,1,64,128]{3,2,1,0:T(8,128)S(1)}, f32[4,1,64,128]{3,2,1,0:T(8,128)S(1)}, u32[]{:S(2)}, u32[]{:S(2)}) collective-permute-start(f32[4,1,64,128]{3,2,1,0:T(8,128)S(1)} %get-tuple-element.1060), channel_id=1, source_target_pairs={{0,4},{4,8},{8,12},{12,16},{16,20},{20,24},{24,28},{28,32},{32,36}... | collective-permute-start | bytes 393224 | tf_op jit(solution)/shard_map/ppermute | solution.py:31
  233.6 6.9 %collective-permute-start.23 = (f32[4,10,1,128]{3,2,1,0:T(1,128)S(1)}, f32[4,10,1,128]{3,2,1,0:T(1,128)S(1)}, u32[]{:S(2)}, u32[]{:S(2)}) collective-permute-start(f32[4,10,1,128]{3,2,1,0:T(1,128)S(1)} %get-tuple-element.1045), channel_id=1, source_target_pairs={{0,1},{1,2},{2,3},{4,5},{5,6},{6,7},{8,9},{9,10},{10,11},{12,13},{... | collective-permute-start | bytes 61448 | tf_op jit(solution)/shard_map/ppermute | solution.py:31
  (51 other events, 317.2 us)
where the time goes:
time: 248 us; the launch traced here: 246 us
  starting transfers between devices  114 us (46%)
  waiting for transfers between devices  55.9 us (23%)
  other arithmetic  36.1 us (15%)
  matrix products  17.3 us (7%)
  local copies, waits for them, and re-layouts  16.7 us (7%)
  between operations  6.03 us (2%)
    ppermute x12, starting transfers between devices, with_halo(): before = lax.ppermute(last, axis, up)  46.1 us
    ppermute x10, starting transfers between devices, shifted_2(): return lax.ppermute(x, axis, pairs)  37.8 us
    ppermute x12, waiting for transfers between devices, with_halo(): before = lax.ppermute(last, axis, up)  34.9 us
    ppermute x12, starting transfers between devices, with_halo(): after = lax.ppermute(leading, axis, down)  29.9 us
    ppermute x12, waiting for transfers between devices, with_halo(): after = lax.ppermute(leading, axis, down)  20.5 us
    dot_general x6, matrix products, ember_update(): jnp.einsum('kxyz,ez->kxye', tile_fields, weight_level, precision=lax.Prec...  11.4 us
    sub x6, other arithmetic, advance(): centre + HORIZONTAL_MIX * spread + VERTICAL_MIX * column_mix  9.19 us
    slice x12, local copies, waits for them, and re-layouts, advance(): lower_level = jnp.concatenate([centre[..., :1], centre[..., :-1]], axis=-1)  8.26 us
  transfers between devices with their start and end apart: 34, of which 14 were waited for; matrix products, arithmetic and copies ran while one was open for 22% of the time, Pallas kernels for 0%

commit v1 on v0

v1 whole, which is shorter than its diff:
```python
import jax
import jax.numpy as jnp
from jax import lax
from jax.experimental import pallas as pl
from jax.experimental.pallas import tpu as pltpu
from jax.sharding import PartitionSpec as P

STEPS = 6
HORIZONTAL_MIX = 0.1
VERTICAL_MIX = 0.1
ADVECTION = 0.25
DRAG_RATE = 0.6
BURN_RATE = 0.5
HEAT_YIELD = 4.0

CX, CY, NZ = 8, 64, 128
CAP = 256
H = STEPS
PAD = 16
WIDE = CY + 2 * PAD
TALL = CX + 2 * H
CORNER = ((1, 0, 5), (3, 5, 3), (2, 8, 4), (4, 12, 2), (5, 14, 1))
REC_ROWS = 24
E1_ROWS = REC_ROWS + 4 * 16
C_COLS = 0
C_CORN = 32
C_RECS = 48
C_ROWS = 52

VMEM = pl.BlockSpec(memory_space=pltpu.VMEM)
SMEM = pl.BlockSpec(memory_space=pltpu.SMEM)
ANY = pl.BlockSpec(memory_space=pl.ANY)


def pack_kernel(counts_ref, fields_ref, embers_ref, e1_ref, f1_ref, e2_ref):
    lane = lax.broadcasted_iota(jnp.int32, (1, CAP), 1)
    for slot in range(6):
        live = (lane < counts_ref[slot]).astype(jnp.float32)
        target = e1_ref if slot < 3 else e2_ref
        for comp in range(7):
            row = comp * 3 + slot % 3
            target[row : row + 1, :] = embers_ref[comp, slot : slot + 1, :] * live
    for k in range(4):
        for dist, first, cols in CORNER:
            at = REC_ROWS + 16 * k + first
            for ref, row in ((e1_ref, CX - dist), (f1_ref, dist - 1)):
                if ref is f1_ref:
                    at = 16 * k + first
                ref[at : at + cols, 0:NZ] = fields_ref[k, row, 0:cols, :]
                ref[at : at + cols, NZ:] = fields_ref[k, row, CY - cols : CY, :]
    zero = jnp.zeros((1, 2 * NZ), jnp.float32)
    for k in range(4):
        f1_ref[16 * k + 15 : 16 * k + 16, :] = zero
        e1_ref[REC_ROWS + 16 * k + 15 : REC_ROWS + 16 * k + 16, :] = zero
    e1_ref[21:24, :] = jnp.zeros((3, 2 * NZ), jnp.float32)
    e2_ref[21:24, :] = jnp.zeros((3, 2 * NZ), jnp.float32)


def turn_kernel(fields_ref, e1_ref, f1_ref, e2_ref, cp_ref, cm_ref):
    for out, side, slot in ((cp_ref, 1, 2), (cm_ref, 0, 0)):
        col = (CY - 8) * side
        for k in range(4):
            for row in range(CX):
                out[C_COLS + 8 * k + row] = fields_ref[k, row, col : col + 8, :]
            for half in range(2):
                at = 16 * k + 8 * half
                lanes = slice(NZ * side, NZ * side + NZ)
                out[C_CORN + 2 * k + half] = e1_ref[REC_ROWS + at : REC_ROWS + at + 8, lanes]
                out[C_CORN + 8 + 2 * k + half] = f1_ref[at : at + 8, lanes]
        for comp in range(7):
            for which, ref in ((0, e1_ref), (1, e2_ref)):
                for half in range(2):
                    row = (comp * 2 + which) * 2 + half
                    out[C_RECS + row // 8, row % 8 : row % 8 + 1, :] = ref[
                        comp * 3 + slot : comp * 3 + slot + 1, NZ * half : NZ * half + NZ
                    ]
        out[C_RECS + 3, 4:8, :] = jnp.zeros((4, NZ), jnp.float32)


def split(x):
    high = x.astype(jnp.bfloat16)
    low = (x - high.astype(jnp.float32)).astype(jnp.bfloat16)
    return high, low


def dot32(a, b):
    return lax.dot_general(a, b, (((1,), (0,)), ((), ())), preferred_element_type=jnp.float32)


def dot32t(a, b):
    return lax.dot_general(a, b, (((1,), (1,)), ((), ())), preferred_element_type=jnp.float32)


def tent(position, count):
    centre = lax.broadcasted_iota(jnp.int32, (count, CAP), 0).astype(jnp.float32) + 0.5
    return jnp.maximum(0.0, 1.0 - jnp.abs(position - centre))


def ember_kernel(
    fields_ref, e1_ref, e2_ref, cp_ref, cm_ref, landed_ref, deposit_ref, rec, parts, weight, fate
):
    cells = CX * CY
    for k in range(4):
        high, low = split(fields_ref[k].reshape(cells, NZ))
        parts[k, :, 0:NZ] = high
        parts[k, :, NZ:] = low
    deposit_ref[...] = jnp.zeros_like(deposit_ref)
    for comp in range(7):
        rec[1, comp : comp + 1, :] = e1_ref[comp * 3 + 1 : comp * 3 + 2, :]
        rec[4, comp : comp + 1, :] = e2_ref[comp * 3 + 1 : comp * 3 + 2, :]
        for which in range(2):
            for half in range(2):
                row = (comp * 2 + which) * 2 + half
                for ref, slot in ((cp_ref, 2), (cm_ref, 0)):
                    rec[3 * which + slot, comp : comp + 1, NZ * half : NZ * half + NZ] = ref[
                        C_RECS + row // 8, row % 8 : row % 8 + 1, :
                    ]

    @pl.loop(0, 6)
    def _(slot):
        field = [rec[slot, i : i + 1, :] for i in range(7)]
        down = tent(field[0] * CX, CX)
        cross = tent(field[1] * CY, CY)
        level = tent(field[2] * NZ, NZ)
        for x in range(CX):
            weight[CY * x : CY * x + CY, :] = down[x : x + 1, :] * cross
        level_high, level_low = split(level)
        both = jnp.concatenate([level_high, level_high], axis=0)
        sampled = []
        for k in range(4):
            column = dot32(parts[k], both) + dot32(parts[k, :, 0:NZ], level_low)
            sampled.append(jnp.sum(column * weight[...], axis=0, keepdims=True))
        mass = field[5]
        heat = field[6] + sampled[2] - sampled[3]
        burned = mass * BURN_RATE * jax.nn.sigmoid(heat)
        living = (mass > 0.0).astype(jnp.float32)
        fate[slot, 0:1, :] = (field[3] + DRAG_RATE * (sampled[0] - field[3])) * living
        fate[slot, 1:2, :] = (field[4] + DRAG_RATE * (sampled[1] - field[4])) * living
        fate[slot, 2:3, :] = (field[6] + DRAG_RATE * (sampled[2] - field[6])) * living
        fate[slot, 3:4, :] = (mass - burned) * living
        heat_high, heat_low = split(level * (HEAT_YIELD * burned))
        weight_high, weight_low = split(weight[...])
        extra = (
            dot32t(weight_high, heat_high)
            + dot32t(weight_high, heat_low)
            + dot32t(weight_low, heat_high)
        )
        deposit_ref[...] += extra

    for slot in range(6):
        for i in range(4):
            landed_ref[i, slot : slot + 1, :] = fate[slot, i : i + 1, :]


def stencil_kernel(
    flags_ref, up_ref, fields_ref, dn_ref, cp_ref, cm_ref, deposit_ref, out_ref, a, b, sems
):
    copies = [
        pltpu.make_async_copy(up_ref, a.at[:, 0:H, PAD : PAD + CY, :], sems.at[0]),
        pltpu.make_async_copy(fields_ref, a.at[:, H : H + CX, PAD : PAD + CY, :], sems.at[1]),
        pltpu.make_async_copy(dn_ref, a.at[:, H + CX :, PAD : PAD + CY, :], sems.at[2]),
    ]
    for copy in copies:
        copy.start()
    zero = jnp.zeros((PAD, NZ), jnp.float32)
    edge = jnp.zeros((8, NZ), jnp.float32)
    for k in range(4):
        for row in range(TALL):
            if H <= row < H + CX:
                a[k, row, 0:8, :] = edge
                a[k, row, 8:16, :] = cp_ref[C_COLS + 8 * k + row - H]
                a[k, row, PAD + CY : PAD + CY + 8, :] = cm_ref[C_COLS + 8 * k + row - H]
                a[k, row, PAD + CY + 8 :, :] = edge
            else:
                a[k, row, 0:PAD, :] = zero
                a[k, row, PAD + CY :, :] = zero
            b[k, row, 0:8, :] = edge
            b[k, row, PAD + CY + 8 :, :] = edge
        for dist, first, cols in CORNER:
            half, at = first // 8, first % 8
            for part, row in ((0, H - dist), (8, H + CX - 1 + dist)):
                entry = C_CORN + part + 2 * k + half
                a[k, row, PAD - cols : PAD, :] = cp_ref[entry, at : at + cols, :]
                a[k, row, PAD + CY : PAD + CY + cols, :] = cm_ref[entry, at : at + cols, :]
    for copy in copies:
        copy.wait()

    lane = lax.broadcasted_iota(jnp.int32, (8, NZ), 1)
    first_level = lane == 0
    last_level = lane == NZ - 1
    left, right = (flags_ref[2].astype(jnp.float32), flags_ref[3].astype(jnp.float32))

    def cell_block(src, row, col, scale):
        half_step = ADVECTION * 0.5 * scale
        mix = HORIZONTAL_MIX * scale
        u = src[0, row, col : col + 8, :] * half_step
        v = src[1, row, col : col + 8, :] * half_step
        east, west, north, south = (mix - u, mix + u, mix - v, mix + v)
        keep = (1.0 - 4.0 * HORIZONTAL_MIX - 2.0 * VERTICAL_MIX) * scale
        column = VERTICAL_MIX * scale
        out = []
        for k in range(4):
            f = src[k, row, col : col + 8, :]
            above = jnp.where(last_level, f, pltpu.roll(f, NZ - 1, 1))
            below = jnp.where(first_level, f, pltpu.roll(f, 1, 1))
            out.append(
                (keep * f + column * (above + below))
                + (east * src[k, row + 1, col : col + 8, :] + west * src[k, row - 1, col : col + 8, :])
                + (
                    north * src[k, row, col + 1 : col + 9, :]
                    + south * src[k, row, col - 1 : col + 7, :]
                )
            )
        return out

    for step in range(1, STEPS):
        src, dst = (a, b) if step % 2 == 1 else (b, a)

        @pl.loop(step, TALL - step)
        def _(row):
            inside = jnp.where(row < H, flags_ref[0], jnp.where(row >= H + CX, flags_ref[1], 1))
            inside = inside.astype(jnp.float32)
            for block in range(10):
                col = 8 + 8 * block
                scale = inside * left if block == 0 else inside * right if block == 9 else inside
                for k, value in enumerate(cell_block(src, row, col, scale)):
                    dst[k, row, col : col + 8, :] = value

    src = a if STEPS % 2 == 1 else b

    @pl.loop(0, CX)
    def _(row):
        for block in range(8):
            col = PAD + 8 * block
            for k, value in enumerate(cell_block(src, row + H, col, 1.0)):
                if k == 2:
                    value = value + deposit_ref[row, 8 * block : 8 * block + 8, :]
                out_ref[k, row, 8 * block : 8 * block + 8, :] = value


def struct(*shape):
    return jax.ShapeDtypeStruct(shape, jnp.float32)


def moved(x, axis, by):
    size = lax.axis_size(axis)
    pairs = [(i, i + by) for i in range(size) if 0 <= i + by < size]
    return lax.ppermute(x, axis, pairs)


PARAMS = pltpu.CompilerParams(vmem_limit_bytes=32 * 1024 * 1024)


def local(fields, embers, counts):
    down, cross = (lax.axis_index("down"), lax.axis_index("cross"))
    flags = jnp.stack(
        [
            down > 0,
            down < lax.axis_size("down") - 1,
            cross > 0,
            cross < lax.axis_size("cross") - 1,
        ]
    ).astype(jnp.int32)
    up = moved(fields[:, CX - H :], "down", 1)
    dn = moved(fields[:, :H], "down", -1)
    e1, f1, e2 = pl.pallas_call(
        pack_kernel,
        out_shape=(struct(E1_ROWS, CAP), struct(64, CAP), struct(REC_ROWS, CAP)),
        in_specs=[SMEM, VMEM, VMEM],
        out_specs=(VMEM, VMEM, VMEM),
        compiler_params=PARAMS,
        name="pack",
    )(counts[0, 0], fields, embers[:, 0, 0])
    e1 = moved(e1, "down", 1)
    f1 = moved(f1, "down", -1)
    e2 = moved(e2, "down", 2)
    cp, cm = pl.pallas_call(
        turn_kernel,
        out_shape=(struct(C_ROWS, 8, NZ), struct(C_ROWS, 8, NZ)),
        in_specs=[VMEM] * 4,
        out_specs=(VMEM, VMEM),
        compiler_params=PARAMS,
        name="turn",
    )(fields, e1, f1, e2)
    cp = moved(cp, "cross", 1)
    cm = moved(cm, "cross", -1)
    landed, deposit = pl.pallas_call(
        ember_kernel,
        out_shape=(struct(4, 6, CAP), struct(CX * CY, NZ)),
        in_specs=[VMEM] * 5,
        out_specs=(VMEM, VMEM),
        scratch_shapes=[
            pltpu.VMEM((6, 8, CAP), jnp.float32),
            pltpu.VMEM((4, CX * CY, 2 * NZ), jnp.bfloat16),
            pltpu.VMEM((CX * CY, CAP), jnp.float32),
            pltpu.VMEM((6, 8, CAP), jnp.float32),
        ],
        compiler_params=PARAMS,
        name="embers",
    )(fields, e1, e2, cp, cm)
    advanced = pl.pallas_call(
        stencil_kernel,
        out_shape=struct(4, CX, CY, NZ),
        in_specs=[SMEM, ANY, ANY, ANY, VMEM, VMEM, VMEM],
        out_specs=VMEM,
        scratch_shapes=[
            pltpu.VMEM((4, TALL, WIDE, NZ), jnp.float32),
            pltpu.VMEM((4, TALL, WIDE, NZ), jnp.float32),
            pltpu.SemaphoreType.DMA((3,)),
        ],
        compiler_params=PARAMS,
        name="stencil",
    )(flags, up, fields, dn, cp, cm, deposit.reshape(CX, CY, NZ))
    return (advanced, landed[:, None, None])


def solution(mesh):
    placed = (
        P(None, "down", "cross", None),
        P(None, "down", "cross", None, None),
        P("down", "cross", None),
    )
    return jax.shard_map(
        local,
        mesh=mesh,
        in_specs=placed,
        out_specs=(P(None, "down", "cross", None), P(None, "down", "cross", None, None)),
        check_vma=False,
    )
```

time: 248 us -> 93 us (0.38)
  starting transfers between devices: 114 us -> 30.2 us
  other arithmetic: 36.1 us -> 0.08 us
  Pallas kernels: 0 us -> 23.1 us
  waiting for transfers between devices: 55.9 us -> 34.5 us
  matrix products: 17.3 us -> 0 us
  local copies, waits for them, and re-layouts: 16.7 us -> 4.09 us
  between operations: 6.03 us -> 0.76 us
    ppermute x34 -> x7, starting transfers between devices: 114 us -> 30.2 us  [moved(): return lax.ppermute(x, axis, pairs)]
    pallas_call x0 -> x4, Pallas kernels: none -> 23.1 us  [the longest x1 14 us: local(): pl.pallas_call(stencil_kernel, out_shape=struct(4, CX, CY, NZ), in_specs=...]
    ppermute x34 -> x7, waiting for transfers between devices: 55.9 us -> 34.5 us  [moved(): return lax.ppermute(x, axis, pairs)]
    dot_general x12 -> x0, matrix products: 17.3 us -> none  [the longest x6 11.4 us: ember_update(): jnp.einsum('kxyz,ez->kxye', tile_fields, weight_level, precision=lax.Prec...]
    mul x34 -> x0, other arithmetic: 13.1 us -> none  [the longest x12 5.05 us: ember_update(): jnp.stack([records[3] + DRAG_RATE * (sampled[0] - records[3]), records[4]...]
    sub x6 -> x0, other arithmetic: 9.19 us -> none  [advance(): centre + HORIZONTAL_MIX * spread + VERTICAL_MIX * column_mix]
    slice x20 -> x1, local copies, waits for them, and re-layouts: 10.1 us -> 2.8 us  [local(): dn = moved(fields[:, :H], 'down', -1)]
    reduce_sum x9 -> x0, other arithmetic: 5.86 us -> none  [the longest x6 4.02 us: local(): live_count = jnp.sum((records[5] > 0.0).astype(jnp.int32))]
  transfers between devices with their start and end apart: 34 -> 7, of which waited for: 14 -> 4; matrix products, arithmetic and copies ran while one was open for 22% -> 1% of each run, Pallas kernels for 0% -> 10%
where the time goes in v1:
time: 93 us; the launch traced here: 92.7 us
  waiting for transfers between devices  34.5 us (37%)
  starting transfers between devices  30.2 us (32%)
  Pallas kernels  23.1 us (25%)
  local copies, waits for them, and re-layouts  4.09 us (4%)
    ppermute x7, waiting for transfers between devices, moved(): return lax.ppermute(x, axis, pairs)  34.5 us
    ppermute x7, starting transfers between devices, moved(): return lax.ppermute(x, axis, pairs)  30.2 us
    pallas_call x1, Pallas kernels, local(): pl.pallas_call(stencil_kernel, out_shape=struct(4, CX, CY, NZ), in_specs=...  14 us
    pallas_call x1, Pallas kernels, local(): pl.pallas_call(ember_kernel, out_shape=(struct(4, 6, CAP), struct(CX * CY...  7.74 us
    slice x1, local copies, waits for them, and re-layouts, local(): dn = moved(fields[:, :H], 'down', -1)  2.8 us
  transfers between devices with their start and end apart: 7, of which 4 were waited for; matrix products, arithmetic and copies ran while one was open for 1% of the time, Pallas kernels for 10%

profile of v1, /device:TPU:7, one launch (start us, length us, event | category | flops | bytes accessed | tf_op | source)
XLA Modules:
  0.0 92.7 jit_solution(16749442744215445507)
XLA Ops:
  0.6 0.0 copy-start
  0.6 0.0 copy-start.2
  0.6 2.8 %fusion = (f32[4,6,64,128]{3,2,1,0:T(8,128)}, f32[4,6,64,128]{3,2,1,0:T(8,128)}) fusion(f32[4,8,64,128]{3,2,1,0:T(8,128)} %fields_ref.7), kind=kLoop, calls=%fused_computation.2 | loop fusion | bytes 3145728 | tf_op jit(solution)/shard_map/slice | solution.py:265
  3.5 10.6 %collective-permute-start.1 = (f32[4,6,64,128]{3,2,1,0:T(8,128)}, f32[4,6,64,128]{3,2,1,0:T(8,128)S(1)}, u32[]{:S(2)}, u32[]{:S(2)}) collective-permute-start(f32[4,6,64,128]{3,2,1,0:T(8,128)} %get-tuple-element.20), channel_id=1, source_target_pairs={{4,0},{8,4},{12,8},{16,12},{20,16},{24,20},{28,24},{32,28},{36,32}... | collective-permute-start | bytes 2359304 | tf_op jit(solution)/shard_map/ppermute | solution.py:248
  14.1 1.9 %collective-permute-start = (f32[4,6,64,128]{3,2,1,0:T(8,128)}, f32[4,6,64,128]{3,2,1,0:T(8,128)S(1)}, u32[]{:S(2)}, u32[]{:S(2)}) collective-permute-start(f32[4,6,64,128]{3,2,1,0:T(8,128)} %get-tuple-element.21), channel_id=1, source_target_pairs={{0,4},{4,8},{8,12},{12,16},{16,20},{20,24},{24,28},{28,32},{32,36}... | collective-permute-start | bytes 2359304 | tf_op jit(solution)/shard_map/ppermute | solution.py:248
  16.0 0.0 copy-done.2
  16.0 0.0 copy-start.1
  16.1 0.0 copy-done
  16.1 0.6 copy-done.1
  16.7 0.6 pack.1
  17.3 1.9 %collective-permute-start.2 = (f32[88,256]{1,0:T(8,128)S(1)}, f32[88,256]{1,0:T(8,128)S(1)}, u32[]{:S(2)}, u32[]{:S(2)}) collective-permute-start(f32[88,256]{1,0:T(8,128)S(1)} %get-tuple-element.9), channel_id=1, source_target_pairs={{0,4},{4,8},{8,12},{12,16},{16,20},{20,24},{24,28},{28,32},{32,36}... | collective-permute-start | bytes 270344 | tf_op jit(solution)/shard_map/ppermute | solution.py:248
  19.2 8.5 %collective-permute-start.3 = (f32[64,256]{1,0:T(8,128)S(1)}, f32[64,256]{1,0:T(8,128)S(1)}, u32[]{:S(2)}, u32[]{:S(2)}) collective-permute-start(f32[64,256]{1,0:T(8,128)S(1)} %get-tuple-element.10), channel_id=1, source_target_pairs={{4,0},{8,4},{12,8},{16,12},{20,16},{24,20},{28,24},{32,28},{36,32}... | collective-permute-start | bytes 196616 | tf_op jit(solution)/shard_map/ppermute | solution.py:248
  27.7 1.9 %collective-permute-start.4 = (f32[24,256]{1,0:T(8,128)S(1)}, f32[24,256]{1,0:T(8,128)S(1)}, u32[]{:S(2)}, u32[]{:S(2)}) collective-permute-start(f32[24,256]{1,0:T(8,128)S(1)} %get-tuple-element.11), channel_id=1, source_target_pairs={{0,8},{4,12},{8,16},{12,20},{16,24},{20,28},{24,32},{28,36},{32,40... | collective-permute-start | bytes 73736 | tf_op jit(solution)/shard_map/ppermute | solution.py:248
  29.7 8.2 %collective-permute-done.4.e2_ref = f32[24,256]{1,0:T(8,128)S(1)} collective-permute-done((f32[24,256]{1,0:T(8,128)S(1)}, f32[24,256]{1,0:T(8,128)S(1)}, u32[]{:S(2)}, u32[]{:S(2)}) %collective-permute-start.4) | collective-permute-done | bytes 24608 | tf_op jit(solution)/shard_map/ppermute | solution.py:248
  37.8 9.5 %collective-permute-done.3.f1_ref = f32[64,256]{1,0:T(8,128)S(1)} collective-permute-done((f32[64,256]{1,0:T(8,128)S(1)}, f32[64,256]{1,0:T(8,128)S(1)}, u32[]{:S(2)}, u32[]{:S(2)}) %collective-permute-start.3) | collective-permute-done | bytes 65568 | tf_op jit(solution)/shard_map/ppermute | solution.py:248
  47.4 12.8 %collective-permute-done.2.e1_ref = f32[88,256]{1,0:T(8,128)S(1)} collective-permute-done((f32[88,256]{1,0:T(8,128)S(1)}, f32[88,256]{1,0:T(8,128)S(1)}, u32[]{:S(2)}, u32[]{:S(2)}) %collective-permute-start.2) | collective-permute-done | bytes 90144 | tf_op jit(solution)/shard_map/ppermute | solution.py:248
  60.2 0.7 turn.1
  60.9 2.3 %collective-permute-start.5 = (f32[52,8,128]{2,1,0:T(8,128)}, f32[52,8,128]{2,1,0:T(8,128)S(1)}, u32[]{:S(2)}, u32[]{:S(2)}) collective-permute-start(f32[52,8,128]{2,1,0:T(8,128)} %get-tuple-element.12), channel_id=1, source_target_pairs={{0,1},{1,2},{2,3},{4,5},{5,6},{6,7},{8,9},{9,10},{10,11},{12,13},{... | collective-permute-start | bytes 638984 | tf_op jit(solution)/shard_map/ppermute | solution.py:248
  63.2 3.1 %collective-permute-start.6 = (f32[52,8,128]{2,1,0:T(8,128)S(1)}, f32[52,8,128]{2,1,0:T(8,128)S(1)}, u32[]{:S(2)}, u32[]{:S(2)}) collective-permute-start(f32[52,8,128]{2,1,0:T(8,128)S(1)} %get-tuple-element.13), channel_id=1, source_target_pairs={{1,0},{2,1},{3,2},{5,4},{6,5},{7,6},{9,8},{10,9},{11,10},{13,12},{... | collective-permute-start | bytes 638984 | tf_op jit(solution)/shard_map/ppermute | solution.py:248
  66.3 0.1 add_convert_fusion.flags_ref
  66.4 0.0 collective-permute-done.5.cp_ref
  66.4 4.0 %collective-permute-done.6.cm_ref = f32[52,8,128]{2,1,0:T(8,128)S(1)} collective-permute-done((f32[52,8,128]{2,1,0:T(8,128)S(1)}, f32[52,8,128]{2,1,0:T(8,128)S(1)}, u32[]{:S(2)}, u32[]{:S(2)}) %collective-permute-start.6) | collective-permute-done | bytes 213024 | tf_op jit(solution)/shard_map/ppermute | solution.py:248
  70.3 7.7 %embers.1 = (f32[4,6,256]{2,1,0:T(8,128)S(1)}, f32[512,128]{1,0:T(8,128)S(1)}) custom-call(f32[4,8,64,128]{3,2,1,0:T(8,128)S(1)} %copy-done, f32[88,256]{1,0:T(8,128)S(1)} %collective-permute-done.2.e1_ref, f32[24,256]{1,0:T(8,128)S(1)} %collective-permute-done.4.e2_ref, f32[52,8,128]{2,1,0:T(8,128)S(1)} %collective-permute-done.5.cp_ref, ...), custom_call_target="tpu_custom_call" | custom-call | tf_op jit(solution)/shard_map/embers/pallas_call | solution.py:287
  78.1 0.6 copy.8
  78.7 0.0 collective-permute-done.1.dn_ref
  78.7 0.0 collective-permute-done.up_ref
  78.7 14.0 %stencil.1 = f32[4,8,64,128]{3,2,1,0:T(8,128)} custom-call(s32[4]{0:T(128)S(1)} %add_convert_fusion.flags_ref, f32[4,6,64,128]{3,2,1,0:T(8,128)S(1)} %collective-permute-done.up_ref, f32[4,8,64,128]{3,2,1,0:T(8,128)S(1)} %copy-done, f32[4,6,64,128]{3,2,1,0:T(8,128)S(1)} %collective-permute-done.1.dn_ref, f32[52,8,128]{2,1,0:T(8,128)S(1)} %collective-permute-done.5.cp_ref, ...), custom_call_target="tpu_custom_call" | custom-call | tf_op jit(solution)/shard_map/stencil/pallas_call | solution.py:301
  (1 shorter events, 0.0 us)
Async XLA Ops:
  0.6 15.4 %copy-start = (f32[4,8,64,128]{3,2,1,0:T(8,128)S(1)}, f32[4,8,64,128]{3,2,1,0:T(8,128)}, u32[]{:S(2)}) copy-start(f32[4,8,64,128]{3,2,1,0:T(8,128)} %fields_ref.7) | copy-start | bytes 3145732
  0.6 15.4 %copy-start.2 = (f32[7,1,1,6,256]{4,2,3,1,0:T(1,128)S(1)}, f32[7,1,1,6,256]{4,2,3,1,0:T(1,128)}, u32[]{:S(2)}) copy-start(f32[7,1,1,6,256]{4,2,3,1,0:T(1,128)} %param.4) | copy-start | bytes 129028
  3.5 75.3 %collective-permute-start.1 = (f32[4,6,64,128]{3,2,1,0:T(8,128)}, f32[4,6,64,128]{3,2,1,0:T(8,128)S(1)}, u32[]{:S(2)}, u32[]{:S(2)}) collective-permute-start(f32[4,6,64,128]{3,2,1,0:T(8,128)} %get-tuple-element.20), channel_id=1, source_target_pairs={{4,0},{8,4},{12,8},{16,12},{20,16},{24,20},{28,24},{32,28},{36,32}... | collective-permute-start | bytes 2359304 | tf_op jit(solution)/shard_map/ppermute | solution.py:248
  14.1 64.6 %collective-permute-start = (f32[4,6,64,128]{3,2,1,0:T(8,128)}, f32[4,6,64,128]{3,2,1,0:T(8,128)S(1)}, u32[]{:S(2)}, u32[]{:S(2)}) collective-permute-start(f32[4,6,64,128]{3,2,1,0:T(8,128)} %get-tuple-element.21), channel_id=1, source_target_pairs={{0,4},{4,8},{8,12},{12,16},{16,20},{20,24},{24,28},{28,32},{32,36}... | collective-permute-start | bytes 2359304 | tf_op jit(solution)/shard_map/ppermute | solution.py:248
  16.0 0.7 copy-start.1
  17.3 42.9 %collective-permute-start.2 = (f32[88,256]{1,0:T(8,128)S(1)}, f32[88,256]{1,0:T(8,128)S(1)}, u32[]{:S(2)}, u32[]{:S(2)}) collective-permute-start(f32[88,256]{1,0:T(8,128)S(1)} %get-tuple-element.9), channel_id=1, source_target_pairs={{0,4},{4,8},{8,12},{12,16},{16,20},{20,24},{24,28},{28,32},{32,36}... | collective-permute-start | bytes 270344 | tf_op jit(solution)/shard_map/ppermute | solution.py:248
  19.2 28.1 %collective-permute-start.3 = (f32[64,256]{1,0:T(8,128)S(1)}, f32[64,256]{1,0:T(8,128)S(1)}, u32[]{:S(2)}, u32[]{:S(2)}) collective-permute-start(f32[64,256]{1,0:T(8,128)S(1)} %get-tuple-element.10), channel_id=1, source_target_pairs={{4,0},{8,4},{12,8},{16,12},{20,16},{24,20},{28,24},{32,28},{36,32}... | collective-permute-start | bytes 196616 | tf_op jit(solution)/shard_map/ppermute | solution.py:248
  27.7 10.1 %collective-permute-start.4 = (f32[24,256]{1,0:T(8,128)S(1)}, f32[24,256]{1,0:T(8,128)S(1)}, u32[]{:S(2)}, u32[]{:S(2)}) collective-permute-start(f32[24,256]{1,0:T(8,128)S(1)} %get-tuple-element.11), channel_id=1, source_target_pairs={{0,8},{4,12},{8,16},{12,20},{16,24},{20,28},{24,32},{28,36},{32,40... | collective-permute-start | bytes 73736 | tf_op jit(solution)/shard_map/ppermute | solution.py:248
  60.9 5.5 %collective-permute-start.5 = (f32[52,8,128]{2,1,0:T(8,128)}, f32[52,8,128]{2,1,0:T(8,128)S(1)}, u32[]{:S(2)}, u32[]{:S(2)}) collective-permute-start(f32[52,8,128]{2,1,0:T(8,128)} %get-tuple-element.12), channel_id=1, source_target_pairs={{0,1},{1,2},{2,3},{4,5},{5,6},{6,7},{8,9},{9,10},{10,11},{12,13},{... | collective-permute-start | bytes 638984 | tf_op jit(solution)/shard_map/ppermute | solution.py:248
  63.2 7.2 %collective-permute-start.6 = (f32[52,8,128]{2,1,0:T(8,128)S(1)}, f32[52,8,128]{2,1,0:T(8,128)S(1)}, u32[]{:S(2)}, u32[]{:S(2)}) collective-permute-start(f32[52,8,128]{2,1,0:T(8,128)S(1)} %get-tuple-element.13), channel_id=1, source_target_pairs={{1,0},{2,1},{3,2},{5,4},{6,5},{7,6},{9,8},{10,9},{11,10},{13,12},{... | collective-permute-start | bytes 638984 | tf_op jit(solution)/shard_map/ppermute | solution.py:248

commit v2 on v1

v2 whole, which is shorter than its diff:
```python
import jax
import jax.numpy as jnp
from jax import lax
from jax.experimental import pallas as pl
from jax.experimental.pallas import tpu as pltpu
from jax.sharding import PartitionSpec as P

STEPS = 6
HORIZONTAL_MIX = 0.1
VERTICAL_MIX = 0.1
ADVECTION = 0.25
DRAG_RATE = 0.6
BURN_RATE = 0.5
HEAT_YIELD = 4.0

CX, CY, NZ = 8, 64, 128
CAP = 256
H = STEPS
NEAR = 3
FAR = H - NEAR
PAD = 16
WIDE = CY + 2 * PAD
TALL = CX + 2 * H
TOP = H - NEAR
CORNER = {1: 0, 3: 5, 2: 8, 4: 12, 5: 14}
E_CORN = 6
C_RECS = 32
C_BLOCKS = 36

HBM = pl.BlockSpec(memory_space=pltpu.HBM)
VMEM = pl.BlockSpec(memory_space=pltpu.VMEM)
SMEM = pl.BlockSpec(memory_space=pltpu.SMEM)
ANY = pl.BlockSpec(memory_space=pl.ANY)


def corner_entry(k, dist, side):
    return (2 * k + CORNER[dist] // 8) * 2 + side


def edge_kernel(
    counts_ref, embers_ref, fields_hbm, cp_ref, cm_ref, own_ref, fields_ref, counts, embers, sems
):
    copies = [
        pltpu.make_async_copy(counts_ref, counts, sems.at[0]),
        pltpu.make_async_copy(embers_ref, embers, sems.at[1]),
        pltpu.make_async_copy(fields_hbm, fields_ref, sems.at[2]),
    ]
    for copy in copies:
        copy.start()
    for copy in copies[:2]:
        copy.wait()
    lane = lax.broadcasted_iota(jnp.int32, (1, NZ), 1)
    for slot in range(6):
        base, target = ((C_RECS, cm_ref), (0, own_ref), (C_RECS, cp_ref))[slot % 3]
        for half in range(2):
            live = (lane + NZ * half < counts[0, 0, slot]).astype(jnp.float32)
            for comp in range(7):
                row = comp * 12 + slot * 2 + half
                put = comp * 4 + slot // 3 * 2 + half
                target[base + put // 8, put % 8 : put % 8 + 1, :] = (
                    embers[row // 4, row % 4 : row % 4 + 1, :] * live
                )
    for base, target in ((C_RECS, cm_ref), (0, own_ref), (C_RECS, cp_ref)):
        target[base + 3, 4:8, :] = jnp.zeros((4, NZ), jnp.float32)
    copies[2].wait()
    for k in range(4):
        for row in range(CX):
            cp_ref[8 * k + row] = fields_ref[k, row, CY - 8 :, :]
            cm_ref[8 * k + row] = fields_ref[k, row, 0:8, :]


def records_kernel(cp_ref, cm_ref, own_ref, e1_ref, f1_ref, e2_ref):
    for which, target in ((0, e1_ref), (1, e2_ref)):
        for j, base, ref in ((0, C_RECS, cm_ref), (1, 0, own_ref), (2, C_RECS, cp_ref)):
            for comp in range(7):
                for half in range(2):
                    row = comp * 4 + which * 2 + half
                    put = comp * 6 + j * 2 + half
                    target[put // 8, put % 8 : put % 8 + 1, :] = ref[
                        base + row // 8, row % 8 : row % 8 + 1, :
                    ]
        target[5, 2:8, :] = jnp.zeros((6, NZ), jnp.float32)
    for k in range(4):
        for ref, base, up in ((e1_ref, E_CORN, True), (f1_ref, 0, False)):
            for dist, first in CORNER.items():
                cols = H - dist
                at = first % 8
                row = CX - dist if up else dist - 1
                ref[base + corner_entry(k, dist, 0), at : at + cols, :] = cp_ref[
                    8 * k + row, 8 - cols : 8, :
                ]
                ref[base + corner_entry(k, dist, 1), at : at + cols, :] = cm_ref[
                    8 * k + row, 0:cols, :
                ]
            for side in range(2):
                ref[base + corner_entry(k, 5, side), 7:8, :] = jnp.zeros((1, NZ), jnp.float32)


def pack_kernel(fields_ref, ua_ref, da_ref, ub_ref, db_ref):
    for k in range(4):
        for i in range(NEAR):
            ua_ref[k, i] = fields_ref[k, CX - NEAR + i]
            da_ref[k, i] = fields_ref[k, i]
        for i in range(FAR):
            ub_ref[k, i] = fields_ref[k, CX - H + i]
            db_ref[k, i] = fields_ref[k, NEAR + i]


def split(x):
    high = x.astype(jnp.bfloat16)
    low = (x - high.astype(jnp.float32)).astype(jnp.bfloat16)
    return high, low


def dot32(a, b):
    return lax.dot_general(a, b, (((1,), (0,)), ((), ())), preferred_element_type=jnp.float32)


def dot32t(a, b):
    return lax.dot_general(a, b, (((1,), (1,)), ((), ())), preferred_element_type=jnp.float32)


def tent(position, count):
    centre = lax.broadcasted_iota(jnp.int32, (count, CAP), 0).astype(jnp.float32) + 0.5
    return jnp.maximum(0.0, 1.0 - jnp.abs(position - centre))


def ember_kernel(
    fields_ref, e1_ref, e2_ref, landed_ref, deposit_ref, rec, parts, weight, fate
):
    cells = CX * CY
    for k in range(4):
        high, low = split(fields_ref[k].reshape(cells, NZ))
        parts[k, :, 0:NZ] = high
        parts[k, :, NZ:] = low
    deposit_ref[...] = jnp.zeros_like(deposit_ref)
    for slot in range(6):
        ref = e1_ref if slot < 3 else e2_ref
        for comp in range(7):
            for half in range(2):
                row = comp * 6 + slot % 3 * 2 + half
                rec[slot, comp : comp + 1, NZ * half : NZ * half + NZ] = ref[
                    row // 8, row % 8 : row % 8 + 1, :
                ]

    @pl.loop(0, 6)
    def _(slot):
        field = [rec[slot, i : i + 1, :] for i in range(7)]
        down = tent(field[0] * CX, CX)
        cross = tent(field[1] * CY, CY)
        level = tent(field[2] * NZ, NZ)
        for x in range(CX):
            weight[CY * x : CY * x + CY, :] = down[x : x + 1, :] * cross
        level_high, level_low = split(level)
        both = jnp.concatenate([level_high, level_high], axis=0)
        sampled = []
        for k in range(4):
            column = dot32(parts[k], both) + dot32(parts[k, :, 0:NZ], level_low)
            sampled.append(jnp.sum(column * weight[...], axis=0, keepdims=True))
        mass = field[5]
        heat = field[6] + sampled[2] - sampled[3]
        burned = mass * BURN_RATE * jax.nn.sigmoid(heat)
        living = (mass > 0.0).astype(jnp.float32)
        fate[slot, 0:1, :] = (field[3] + DRAG_RATE * (sampled[0] - field[3])) * living
        fate[slot, 1:2, :] = (field[4] + DRAG_RATE * (sampled[1] - field[4])) * living
        fate[slot, 2:3, :] = (field[6] + DRAG_RATE * (sampled[2] - field[6])) * living
        fate[slot, 3:4, :] = (mass - burned) * living
        heat_high, heat_low = split(level * (HEAT_YIELD * burned))
        weight_high, weight_low = split(weight[...])
        extra = (
            dot32t(weight_high, heat_high)
            + dot32t(weight_high, heat_low)
            + dot32t(weight_low, heat_high)
        )
        deposit_ref[...] += extra

    for slot in range(6):
        for i in range(4):
            for half in range(2):
                row = i * 12 + slot * 2 + half
                landed_ref[row // 4, row % 4 : row % 4 + 1, :] = fate[
                    slot, i : i + 1, NZ * half : NZ * half + NZ
                ]


def edges():
    lane = lax.broadcasted_iota(jnp.int32, (8, NZ), 1)
    return lane == 0, lane == NZ - 1


def cell_block(src, row, col, scale, ends):
    first_level, last_level = ends
    half_step = ADVECTION * 0.5 * scale
    mix = HORIZONTAL_MIX * scale
    u = src[0, row, col : col + 8, :] * half_step
    v = src[1, row, col : col + 8, :] * half_step
    east, west, north, south = (mix - u, mix + u, mix - v, mix + v)
    keep = (1.0 - 4.0 * HORIZONTAL_MIX - 2.0 * VERTICAL_MIX) * scale
    column = VERTICAL_MIX * scale
    out = []
    for k in range(4):
        f = src[k, row, col : col + 8, :]
        above = jnp.where(last_level, f, pltpu.roll(f, NZ - 1, 1))
        below = jnp.where(first_level, f, pltpu.roll(f, 1, 1))
        out.append(
            (keep * f + column * (above + below))
            + (east * src[k, row + 1, col : col + 8, :] + west * src[k, row - 1, col : col + 8, :])
            + (
                north * src[k, row, col + 1 : col + 9, :]
                + south * src[k, row, col - 1 : col + 7, :]
            )
        )
    return out


def wide_row(flags_ref, src, dst, row, ends):
    inside = jnp.where(row < H, flags_ref[0], jnp.where(row >= H + CX, flags_ref[1], 1))
    inside = inside.astype(jnp.float32)
    left, right = (flags_ref[2].astype(jnp.float32), flags_ref[3].astype(jnp.float32))
    for block in range(10):
        col = 8 + 8 * block
        scale = inside * left if block == 0 else inside * right if block == 9 else inside
        for k, value in enumerate(cell_block(src, row, col, scale, ends)):
            dst[k, row, col : col + 8, :] = value


def fill_sides(a, rows, e1_ref, f1_ref):
    zero = jnp.zeros((PAD, NZ), jnp.float32)
    for k in range(4):
        for row in rows:
            a[k, row, 0:PAD, :] = zero
            a[k, row, PAD + CY :, :] = zero
            ref, base, dist = (e1_ref, E_CORN, H - row)
            if row >= H:
                ref, base, dist = (f1_ref, 0, row - (H + CX - 1))
            if dist in CORNER:
                cols, at = H - dist, CORNER[dist] % 8
                a[k, row, PAD - cols : PAD, :] = ref[
                    base + corner_entry(k, dist, 0), at : at + cols, :
                ]
                a[k, row, PAD + CY : PAD + CY + cols, :] = ref[
                    base + corner_entry(k, dist, 1), at : at + cols, :
                ]


def near_kernel(
    flags_ref, fields_ref, ua_ref, da_ref, cp_ref, cm_ref, e1_ref, f1_ref, a, b, sem
):
    copy = pltpu.make_async_copy(fields_ref, a.at[:, H : H + CX, PAD : PAD + CY, :], sem)
    copy.start()
    edge = jnp.zeros((8, NZ), jnp.float32)
    for k in range(4):
        for row in range(CX):
            a[k, H + row, 0:8, :] = edge
            a[k, H + row, 8:16, :] = cp_ref[8 * k + row]
            a[k, H + row, PAD + CY : PAD + CY + 8, :] = cm_ref[8 * k + row]
            a[k, H + row, PAD + CY + 8 :, :] = edge
        for i in range(NEAR):
            a[k, TOP + i, PAD : PAD + CY, :] = ua_ref[k, i]
            a[k, H + CX + i, PAD : PAD + CY, :] = da_ref[k, i]
        for row in range(TALL):
            b[k, row, 0:8, :] = edge
            b[k, row, PAD + CY + 8 :, :] = edge
    fill_sides(a, (*range(TOP, H), *range(H + CX, H + CX + NEAR)), e1_ref, f1_ref)
    copy.wait()
    ends = edges()
    for step in range(1, STEPS + 1):
        src, dst = (a, b) if step % 2 == 1 else (b, a)
        if TOP + step < TALL - TOP - step:

            @pl.loop(TOP + step, TALL - TOP - step)
            def _(row):
                wide_row(flags_ref, src, dst, row, ends)


def far_kernel(
    flags_ref, ub_ref, db_ref, e1_ref, f1_ref, deposit_ref, a_in, b_in, out_ref, a, b
):
    fill_sides(a, (*range(FAR), *range(TALL - FAR, TALL)), e1_ref, f1_ref)
    for k in range(4):
        for i in range(FAR):
            a[k, i, PAD : PAD + CY, :] = ub_ref[k, i]
            a[k, TALL - FAR + i, PAD : PAD + CY, :] = db_ref[k, i]
    ends = edges()
    for step in range(1, STEPS):
        src, dst = (a, b) if step % 2 == 1 else (b, a)

        @pl.loop(0, FAR)
        def _(i):
            wide_row(flags_ref, src, dst, i + step, ends)
            wide_row(flags_ref, src, dst, TALL - 1 - step - i, ends)

    src, dst = (a, b) if STEPS % 2 == 1 else (b, a)

    def last_row(row, values):
        for block in range(8):
            for k, value in enumerate(values(row, PAD + 8 * block)):
                if k == 2:
                    value = value + deposit_ref[row, 8 * block : 8 * block + 8, :]
                out_ref[k, row, 8 * block : 8 * block + 8, :] = value

    def computed(row, col):
        return cell_block(src, row + H, col, 1.0, ends)

    def kept(row, col):
        return [dst[k, row + H, col : col + 8, :] for k in range(4)]

    done = range(H - NEAR, NEAR + CX - H)
    if len(done):

        @pl.loop(0, done.start)
        def _(row):
            last_row(row, computed)
            last_row(CX - 1 - row, computed)

        for row in done:
            last_row(row, kept)
    else:

        @pl.loop(0, CX)
        def _(row):
            last_row(row, computed)


def struct(*shape):
    return jax.ShapeDtypeStruct(shape, jnp.float32)


def moved(x, axis, by):
    size = lax.axis_size(axis)
    pairs = [(i, i + by) for i in range(size) if 0 <= i + by < size]
    return lax.ppermute(x, axis, pairs)


PARAMS = pltpu.CompilerParams(vmem_limit_bytes=32 * 1024 * 1024)


def local(fields, embers, counts):
    down, cross = (lax.axis_index("down"), lax.axis_index("cross"))
    flags = jnp.stack(
        [
            down > 0,
            down < lax.axis_size("down") - 1,
            cross > 0,
            cross < lax.axis_size("cross") - 1,
        ]
    ).astype(jnp.int32)
    cp, cm, own, fields = pl.pallas_call(
        edge_kernel,
        out_shape=(
            struct(C_BLOCKS, 8, NZ),
            struct(C_BLOCKS, 8, NZ),
            struct(4, 8, NZ),
            struct(4, CX, CY, NZ),
        ),
        in_specs=[HBM, HBM, HBM],
        out_specs=(VMEM,) * 4,
        scratch_shapes=[
            pltpu.SMEM((1, 1, 6), jnp.int32),
            pltpu.VMEM((21, 4, NZ), jnp.float32),
            pltpu.SemaphoreType.DMA((3,)),
        ],
        compiler_params=PARAMS,
        name="edges",
    )(counts, embers.reshape(21, 4, NZ), fields)
    cp = moved(cp, "cross", 1)
    cm = moved(cm, "cross", -1)
    ua, da, ub, db = pl.pallas_call(
        pack_kernel,
        out_shape=(
            struct(4, NEAR, CY, NZ),
            struct(4, NEAR, CY, NZ),
            struct(4, FAR, CY, NZ),
            struct(4, FAR, CY, NZ),
        ),
        in_specs=[VMEM],
        out_specs=(VMEM,) * 4,
        compiler_params=PARAMS,
        name="pack",
    )(fields)
    ua = moved(ua, "down", 1)
    da = moved(da, "down", -1)
    e1, f1, e2 = pl.pallas_call(
        records_kernel,
        out_shape=(struct(E_CORN + 16, 8, NZ), struct(16, 8, NZ), struct(6, 8, NZ)),
        in_specs=[VMEM] * 3,
        out_specs=(VMEM,) * 3,
        compiler_params=PARAMS,
        name="records",
    )(cp, cm, own)
    e1 = moved(e1, "down", 1)
    f1 = moved(f1, "down", -1)
    e2 = moved(e2, "down", 2)
    ub, db, e1, f1, e2 = lax.optimization_barrier((ub, db, e1, f1, e2))
    ub = moved(ub, "down", 1)
    db = moved(db, "down", -1)
    landed, deposit = pl.pallas_call(
        ember_kernel,
        out_shape=(struct(12, 4, NZ), struct(CX * CY, NZ)),
        in_specs=[VMEM] * 3,
        out_specs=(VMEM, VMEM),
        scratch_shapes=[
            pltpu.VMEM((6, 8, CAP), jnp.float32),
            pltpu.VMEM((4, CX * CY, 2 * NZ), jnp.bfloat16),
            pltpu.VMEM((CX * CY, CAP), jnp.float32),
            pltpu.VMEM((6, 8, CAP), jnp.float32),
        ],
        compiler_params=PARAMS,
        name="embers",
    )(fields, e1, e2)
    tile = struct(4, TALL, WIDE, NZ)
    a, b = pl.pallas_call(
        near_kernel,
        out_shape=(tile, tile),
        in_specs=[SMEM, ANY] + [VMEM] * 6,
        out_specs=(VMEM, VMEM),
        scratch_shapes=[pltpu.SemaphoreType.DMA],
        compiler_params=PARAMS,
        name="near",
    )(flags, fields, ua, da, cp, cm, e1, f1)
    advanced, _, _ = pl.pallas_call(
        far_kernel,
        out_shape=(struct(4, CX, CY, NZ), tile, tile),
        in_specs=[SMEM] + [VMEM] * 7,
        out_specs=(VMEM, VMEM, VMEM),
        input_output_aliases={6: 1, 7: 2},
        compiler_params=PARAMS,
        name="far",
    )(flags, ub, db, e1, f1, deposit.reshape(CX, CY, NZ), a, b)
    return (advanced, landed.reshape(4, 1, 1, 6, CAP))


def solution(mesh):
    placed = (
        P(None, "down", "cross", None),
        P(None, "down", "cross", None, None),
        P("down", "cross", None),
    )
    return jax.shard_map(
        local,
        mesh=mesh,
        in_specs=placed,
        out_specs=(P(None, "down", "cross", None), P(None, "down", "cross", None, None)),
        check_vma=False,
    )
```

time: 93 us -> 76.7 us (0.82)
  the two profiles are of different devices: /device:TPU:7 before, /device:TPU:120 now
where the time goes in v2:
time: 76.7 us; the launch traced here: 76.3 us
  starting transfers between devices  34.7 us (45%)
  Pallas kernels  23.4 us (31%)
  waiting for transfers between devices  14.7 us (19%)
  local copies, waits for them, and re-layouts  2.66 us (3%)
  between operations  0.77 us (1%)
    ppermute x9, starting transfers between devices, moved(): return lax.ppermute(x, axis, pairs)  34.7 us
    ppermute x9, waiting for transfers between devices, moved(): return lax.ppermute(x, axis, pairs)  14.7 us
    pallas_call x1, Pallas kernels, local(): pl.pallas_call(ember_kernel, out_shape=(struct(12, 4, NZ), struct(CX * CY...  8.35 us
    pallas_call x1, Pallas kernels, local(): pl.pallas_call(near_kernel, out_shape=(tile, tile), in_specs=[SMEM, ANY]...  7.4 us
    pallas_call x1, Pallas kernels, local(): pl.pallas_call(far_kernel, out_shape=(struct(4, CX, CY, NZ), tile, tile),...  5.9 us
    unnamed x6, local copies, waits for them, and re-layouts  2.66 us
  transfers between devices with their start and end apart: 9, of which 4 were waited for; matrix products, arithmetic and copies ran while one was open for 0% of the time, Pallas kernels for 22%

profile of v2, /device:TPU:120, one launch (start us, length us, event | category | flops | bytes accessed | tf_op | source)
XLA Modules:
  0.0 76.3 jit_solution(16595995368774965192)
XLA Ops:
  0.6 0.0 copy-start
  0.6 1.2 %copy-done = f32[4,8,64,128]{3,2,1,0:T(8,128)S(1)} copy-done((f32[4,8,64,128]{3,2,1,0:T(8,128)S(1)}, f32[4,8,64,128]{3,2,1,0:T(8,128)}, u32[]{:S(2)}) %copy-start) | copy-done | bytes 1048600
  1.9 0.0 copy-start.1
  1.9 0.8 %copy-done.1 = f32[7,1,1,6,256]{4,2,3,1,0:T(1,128)S(1)} copy-done((f32[7,1,1,6,256]{4,2,3,1,0:T(1,128)S(1)}, f32[7,1,1,6,256]{4,2,3,1,0:T(1,128)}, u32[]{:S(2)}) %copy-start.1) | copy-done | bytes 43032
  2.6 0.0 copy-start.2
  2.6 0.7 copy-done.2
  3.3 0.6 edges.1
  3.9 1.9 %collective-permute-start = (f32[36,8,128]{2,1,0:T(8,128)S(1)}, f32[36,8,128]{2,1,0:T(8,128)S(1)}, u32[]{:S(2)}, u32[]{:S(2)}) collective-permute-start(f32[36,8,128]{2,1,0:T(8,128)S(1)} %get-tuple-element.26), channel_id=1, source_target_pairs={{0,1},{1,2},{2,3},{4,5},{5,6},{6,7},{8,9},{9,10},{10,11},{12,13},{... | collective-permute-start | bytes 442376 | tf_op jit(solution)/shard_map/ppermute | solution.py:332
  5.9 3.6 %collective-permute-start.1 = (f32[36,8,128]{2,1,0:T(8,128)S(1)}, f32[36,8,128]{2,1,0:T(8,128)S(1)}, u32[]{:S(2)}, u32[]{:S(2)}) collective-permute-start(f32[36,8,128]{2,1,0:T(8,128)S(1)} %get-tuple-element.27), channel_id=1, source_target_pairs={{1,0},{2,1},{3,2},{5,4},{6,5},{7,6},{9,8},{10,9},{11,10},{13,12},{... | collective-permute-start | bytes 442376 | tf_op jit(solution)/shard_map/ppermute | solution.py:332
  9.5 0.9 %collective-permute-done.cp_ref = f32[36,8,128]{2,1,0:T(8,128)S(1)} collective-permute-done((f32[36,8,128]{2,1,0:T(8,128)S(1)}, f32[36,8,128]{2,1,0:T(8,128)S(1)}, u32[]{:S(2)}, u32[]{:S(2)}) %collective-permute-start) | collective-permute-done | bytes 147488 | tf_op jit(solution)/shard_map/ppermute | solution.py:332
  10.4 1.8 %collective-permute-done.1.cm_ref = f32[36,8,128]{2,1,0:T(8,128)S(1)} collective-permute-done((f32[36,8,128]{2,1,0:T(8,128)S(1)}, f32[36,8,128]{2,1,0:T(8,128)S(1)}, u32[]{:S(2)}, u32[]{:S(2)}) %collective-permute-start.1) | collective-permute-done | bytes 147488 | tf_op jit(solution)/shard_map/ppermute | solution.py:332
  12.2 5.2 %collective-permute-start.2 = (f32[22,8,128]{2,1,0:T(8,128)S(1)}, f32[22,8,128]{2,1,0:T(8,128)S(1)}, u32[]{:S(2)}, u32[]{:S(2)}) collective-permute-start(f32[22,8,128]{2,1,0:T(8,128)S(1)} %get-tuple-element.29), channel_id=1, source_target_pairs={{0,4},{4,8},{8,12},{12,16},{16,20},{20,24},{24,28},{28,32},{32,36}... | collective-permute-start | bytes 270344 | tf_op jit(solution)/shard_map/ppermute | solution.py:332
  17.4 1.9 %collective-permute-start.3 = (f32[16,8,128]{2,1,0:T(8,128)S(1)}, f32[16,8,128]{2,1,0:T(8,128)S(1)}, u32[]{:S(2)}, u32[]{:S(2)}) collective-permute-start(f32[16,8,128]{2,1,0:T(8,128)S(1)} %get-tuple-element.30), channel_id=1, source_target_pairs={{4,0},{8,4},{12,8},{16,12},{20,16},{24,20},{28,24},{32,28},{36,32}... | collective-permute-start | bytes 196616 | tf_op jit(solution)/shard_map/ppermute | solution.py:332
  19.3 4.9 %collective-permute-start.4 = (f32[6,8,128]{2,1,0:T(8,128)S(1)}, f32[6,8,128]{2,1,0:T(8,128)S(1)}, u32[]{:S(2)}, u32[]{:S(2)}) collective-permute-start(f32[6,8,128]{2,1,0:T(8,128)S(1)} %get-tuple-element.31), channel_id=1, source_target_pairs={{0,8},{4,12},{8,16},{12,20},{16,24},{20,28},{24,32},{28,36},{32,40... | collective-permute-start | bytes 73736 | tf_op jit(solution)/shard_map/ppermute | solution.py:332
  24.2 1.1 %pack.1 = (f32[4,3,64,128]{3,2,1,0:T(8,128)}, f32[4,3,64,128]{3,2,1,0:T(8,128)}, f32[4,3,64,128]{3,2,1,0:T(8,128)}, f32[4,3,64,128]{3,2,1,0:T(8,128)S(1)}) custom-call(f32[4,8,64,128]{3,2,1,0:T(8,128)S(1)} %get-tuple-element.23.fields_ref), custom_call_target="tpu_custom_call" | custom-call | tf_op jit(solution)/shard_map/pack/pallas_call | solution.py:368
  25.3 5.1 %collective-permute-start.7 = (f32[4,3,64,128]{3,2,1,0:T(8,128)}, f32[4,3,64,128]{3,2,1,0:T(8,128)S(1)}, u32[]{:S(2)}, u32[]{:S(2)}) collective-permute-start(f32[4,3,64,128]{3,2,1,0:T(8,128)} %get-tuple-element.38), channel_id=1, source_target_pairs={{0,4},{4,8},{8,12},{12,16},{16,20},{20,24},{24,28},{28,32},{32,36}... | collective-permute-start | bytes 1179656 | tf_op jit(solution)/shard_map/ppermute | solution.py:332
  30.5 2.8 %collective-permute-start.8 = (f32[4,3,64,128]{3,2,1,0:T(8,128)}, f32[4,3,64,128]{3,2,1,0:T(8,128)S(1)}, u32[]{:S(2)}, u32[]{:S(2)}) collective-permute-start(f32[4,3,64,128]{3,2,1,0:T(8,128)} %get-tuple-element.39), channel_id=1, source_target_pairs={{4,0},{8,4},{12,8},{16,12},{20,16},{24,20},{28,24},{32,28},{36,32}... | collective-permute-start | bytes 1179656 | tf_op jit(solution)/shard_map/ppermute | solution.py:332
  33.2 0.0 collective-permute-done.4.e2_ref
  33.2 0.0 collective-permute-done.3.f1_ref
  33.3 0.0 collective-permute-done.2.e1_ref
  33.3 7.3 %collective-permute-start.5 = (f32[4,3,64,128]{3,2,1,0:T(8,128)}, f32[4,3,64,128]{3,2,1,0:T(8,128)S(1)}, u32[]{:S(2)}, u32[]{:S(2)}) collective-permute-start(f32[4,3,64,128]{3,2,1,0:T(8,128)} %get-tuple-element.32), channel_id=1, source_target_pairs={{0,4},{4,8},{8,12},{12,16},{16,20},{20,24},{24,28},{28,32},{32,36}... | collective-permute-start | bytes 1179656 | tf_op jit(solution)/shard_map/ppermute | solution.py:332
  40.6 1.9 %collective-permute-start.6 = (f32[4,3,64,128]{3,2,1,0:T(8,128)S(1)}, f32[4,3,64,128]{3,2,1,0:T(8,128)S(1)}, u32[]{:S(2)}, u32[]{:S(2)}) collective-permute-start(f32[4,3,64,128]{3,2,1,0:T(8,128)S(1)} %get-tuple-element.33), channel_id=1, source_target_pairs={{4,0},{8,4},{12,8},{16,12},{20,16},{24,20},{28,24},{32,28},{36,32}... | collective-permute-start | bytes 1179656 | tf_op jit(solution)/shard_map/ppermute | solution.py:332
  42.5 0.1 add_convert_fusion.flags_ref
  42.6 8.4 %embers.1 = (f32[12,4,128]{2,1,0:T(4,128)}, f32[512,128]{1,0:T(8,128)S(1)}) custom-call(f32[4,8,64,128]{3,2,1,0:T(8,128)S(1)} %get-tuple-element.23.fields_ref, f32[22,8,128]{2,1,0:T(8,128)S(1)} %collective-permute-done.2.e1_ref, f32[6,8,128]{2,1,0:T(8,128)S(1)} %collective-permute-done.4.e2_ref), custom_call_target="tpu_custom_call" | custom-call | tf_op jit(solution)/shard_map/embers/pallas_call | solution.py:397
  50.9 0.0 collective-permute-done.7.ua_ref
  50.9 0.0 collective-permute-done.8.da_ref
  50.9 7.4 %near.1 = (f32[4,20,96,128]{3,2,1,0:T(8,128)S(1)}, f32[4,20,96,128]{3,2,1,0:T(8,128)S(1)}) custom-call(s32[4]{0:T(128)S(1)} %add_convert_fusion.flags_ref, f32[4,8,64,128]{3,2,1,0:T(8,128)S(1)} %get-tuple-element.23.fields_ref, f32[4,3,64,128]{3,2,1,0:T(8,128)S(1)} %collective-permute-done.7.ua_ref, f32[4,3,64,128]{3,2,1,0:T(8,128)S(1)} %collective-permute-done.8.da_ref, ...), custom_call_target="tpu_custom_call" | custom-call | tf_op jit(solution)/shard_map/near/pallas_call | solution.py:412
  58.4 3.0 %collective-permute-done.5.ub_ref = f32[4,3,64,128]{3,2,1,0:T(8,128)S(1)} collective-permute-done((f32[4,3,64,128]{3,2,1,0:T(8,128)}, f32[4,3,64,128]{3,2,1,0:T(8,128)S(1)}, u32[]{:S(2)}, u32[]{:S(2)}) %collective-permute-start.5) | collective-permute-done | bytes 393248 | tf_op jit(solution)/shard_map/ppermute | solution.py:332
  61.3 9.1 %collective-permute-done.6.db_ref = f32[4,3,64,128]{3,2,1,0:T(8,128)S(1)} collective-permute-done((f32[4,3,64,128]{3,2,1,0:T(8,128)S(1)}, f32[4,3,64,128]{3,2,1,0:T(8,128)S(1)}, u32[]{:S(2)}, u32[]{:S(2)}) %collective-permute-start.6) | collective-permute-done | bytes 393248 | tf_op jit(solution)/shard_map/ppermute | solution.py:332
  70.4 5.9 %far.1 = (f32[4,8,64,128]{3,2,1,0:T(8,128)}, f32[4,20,96,128]{3,2,1,0:T(8,128)S(1)}, f32[4,20,96,128]{3,2,1,0:T(8,128)S(1)}) custom-call(s32[4]{0:T(128)S(1)} %add_convert_fusion.flags_ref, f32[4,3,64,128]{3,2,1,0:T(8,128)S(1)} %collective-permute-done.5.ub_ref, ...), custom_call_target="tpu_custom_call", output_to_operand_aliasing={{1}: (6, {}), {2}: (7, {})} | custom-call | tf_op jit(solution)/shard_map/far/pallas_call | solution.py:421
  (1 shorter events, 0.0 us)
Async XLA Ops:
  0.6 1.2 %copy-start = (f32[4,8,64,128]{3,2,1,0:T(8,128)S(1)}, f32[4,8,64,128]{3,2,1,0:T(8,128)}, u32[]{:S(2)}) copy-start(f32[4,8,64,128]{3,2,1,0:T(8,128)} %fields_hbm.1) | copy-start | bytes 3145732
  1.9 0.8 %copy-start.1 = (f32[7,1,1,6,256]{4,2,3,1,0:T(1,128)S(1)}, f32[7,1,1,6,256]{4,2,3,1,0:T(1,128)}, u32[]{:S(2)}) copy-start(f32[7,1,1,6,256]{4,2,3,1,0:T(1,128)} %param.4) | copy-start | bytes 129028
  2.6 0.7 copy-start.2
  3.9 6.5 %collective-permute-start = (f32[36,8,128]{2,1,0:T(8,128)S(1)}, f32[36,8,128]{2,1,0:T(8,128)S(1)}, u32[]{:S(2)}, u32[]{:S(2)}) collective-permute-start(f32[36,8,128]{2,1,0:T(8,128)S(1)} %get-tuple-element.26), channel_id=1, source_target_pairs={{0,1},{1,2},{2,3},{4,5},{5,6},{6,7},{8,9},{9,10},{10,11},{12,13},{... | collective-permute-start | bytes 442376 | tf_op jit(solution)/shard_map/ppermute | solution.py:332
  5.9 6.3 %collective-permute-start.1 = (f32[36,8,128]{2,1,0:T(8,128)S(1)}, f32[36,8,128]{2,1,0:T(8,128)S(1)}, u32[]{:S(2)}, u32[]{:S(2)}) collective-permute-start(f32[36,8,128]{2,1,0:T(8,128)S(1)} %get-tuple-element.27), channel_id=1, source_target_pairs={{1,0},{2,1},{3,2},{5,4},{6,5},{7,6},{9,8},{10,9},{11,10},{13,12},{... | collective-permute-start | bytes 442376 | tf_op jit(solution)/shard_map/ppermute | solution.py:332
  12.2 21.1 %collective-permute-start.2 = (f32[22,8,128]{2,1,0:T(8,128)S(1)}, f32[22,8,128]{2,1,0:T(8,128)S(1)}, u32[]{:S(2)}, u32[]{:S(2)}) collective-permute-start(f32[22,8,128]{2,1,0:T(8,128)S(1)} %get-tuple-element.29), channel_id=1, source_target_pairs={{0,4},{4,8},{8,12},{12,16},{16,20},{20,24},{24,28},{28,32},{32,36}... | collective-permute-start | bytes 270344 | tf_op jit(solution)/shard_map/ppermute | solution.py:332
  17.4 15.9 %collective-permute-start.3 = (f32[16,8,128]{2,1,0:T(8,128)S(1)}, f32[16,8,128]{2,1,0:T(8,128)S(1)}, u32[]{:S(2)}, u32[]{:S(2)}) collective-permute-start(f32[16,8,128]{2,1,0:T(8,128)S(1)} %get-tuple-element.30), channel_id=1, source_target_pairs={{4,0},{8,4},{12,8},{16,12},{20,16},{24,20},{28,24},{32,28},{36,32}... | collective-permute-start | bytes 196616 | tf_op jit(solution)/shard_map/ppermute | solution.py:332
  19.3 13.9 %collective-permute-start.4 = (f32[6,8,128]{2,1,0:T(8,128)S(1)}, f32[6,8,128]{2,1,0:T(8,128)S(1)}, u32[]{:S(2)}, u32[]{:S(2)}) collective-permute-start(f32[6,8,128]{2,1,0:T(8,128)S(1)} %get-tuple-element.31), channel_id=1, source_target_pairs={{0,8},{4,12},{8,16},{12,20},{16,24},{20,28},{24,32},{28,36},{32,40... | collective-permute-start | bytes 73736 | tf_op jit(solution)/shard_map/ppermute | solution.py:332
  25.3 25.6 %collective-permute-start.7 = (f32[4,3,64,128]{3,2,1,0:T(8,128)}, f32[4,3,64,128]{3,2,1,0:T(8,128)S(1)}, u32[]{:S(2)}, u32[]{:S(2)}) collective-permute-start(f32[4,3,64,128]{3,2,1,0:T(8,128)} %get-tuple-element.38), channel_id=1, source_target_pairs={{0,4},{4,8},{8,12},{12,16},{16,20},{20,24},{24,28},{28,32},{32,36}... | collective-permute-start | bytes 1179656 | tf_op jit(solution)/shard_map/ppermute | solution.py:332
  30.5 20.5 %collective-permute-start.8 = (f32[4,3,64,128]{3,2,1,0:T(8,128)}, f32[4,3,64,128]{3,2,1,0:T(8,128)S(1)}, u32[]{:S(2)}, u32[]{:S(2)}) collective-permute-start(f32[4,3,64,128]{3,2,1,0:T(8,128)} %get-tuple-element.39), channel_id=1, source_target_pairs={{4,0},{8,4},{12,8},{16,12},{20,16},{24,20},{28,24},{32,28},{36,32}... | collective-permute-start | bytes 1179656 | tf_op jit(solution)/shard_map/ppermute | solution.py:332
  33.3 28.1 %collective-permute-start.5 = (f32[4,3,64,128]{3,2,1,0:T(8,128)}, f32[4,3,64,128]{3,2,1,0:T(8,128)S(1)}, u32[]{:S(2)}, u32[]{:S(2)}) collective-permute-start(f32[4,3,64,128]{3,2,1,0:T(8,128)} %get-tuple-element.32), channel_id=1, source_target_pairs={{0,4},{4,8},{8,12},{12,16},{16,20},{20,24},{24,28},{28,32},{32,36}... | collective-permute-start | bytes 1179656 | tf_op jit(solution)/shard_map/ppermute | solution.py:332
  40.6 29.8 %collective-permute-start.6 = (f32[4,3,64,128]{3,2,1,0:T(8,128)S(1)}, f32[4,3,64,128]{3,2,1,0:T(8,128)S(1)}, u32[]{:S(2)}, u32[]{:S(2)}) collective-permute-start(f32[4,3,64,128]{3,2,1,0:T(8,128)S(1)} %get-tuple-element.33), channel_id=1, source_target_pairs={{4,0},{8,4},{12,8},{16,12},{20,16},{24,20},{28,24},{32,28},{36,32}... | collective-permute-start | bytes 1179656 | tf_op jit(solution)/shard_map/ppermute | solution.py:332

commit v3 on v2

--- a/solution.py
+++ b/solution.py
@@ -23,7 +23,8 @@
 TALL = CX + 2 * H
 TOP = H - NEAR
 CORNER = {1: 0, 3: 5, 2: 8, 4: 12, 5: 14}
-E_CORN = 6
+B_CORN = 32 * NEAR
+A_BLOCKS = B_CORN + 16
 C_RECS = 32
 C_BLOCKS = 36
 
@@ -34,7 +35,7 @@
 
 
 def corner_entry(k, dist, side):
-    return (2 * k + CORNER[dist] // 8) * 2 + side
+    return B_CORN + (2 * k + CORNER[dist] // 8) * 2 + side
 
 
 def edge_kernel(
@@ -69,7 +70,7 @@
             cm_ref[8 * k + row] = fields_ref[k, row, 0:8, :]
 
 
-def records_kernel(cp_ref, cm_ref, own_ref, e1_ref, f1_ref, e2_ref):
+def records_kernel(cp_ref, cm_ref, own_ref, e1_ref, e2_ref):
     for which, target in ((0, e1_ref), (1, e2_ref)):
         for j, base, ref in ((0, C_RECS, cm_ref), (1, 0, own_ref), (2, C_RECS, cp_ref)):
             for comp in range(7):
@@ -80,27 +81,26 @@
                         base + row // 8, row % 8 : row % 8 + 1, :
                     ]
         target[5, 2:8, :] = jnp.zeros((6, NZ), jnp.float32)
-    for k in range(4):
-        for ref, base, up in ((e1_ref, E_CORN, True), (f1_ref, 0, False)):
+
+
+def pack_kernel(fields_ref, cp_ref, cm_ref, ua_ref, da_ref, ub_ref, db_ref):
+    for k in range(4):
+        for i in range(NEAR):
+            for j in range(8):
+                at = (k * NEAR + i) * 8 + j
+                ua_ref[at] = fields_ref[k, CX - NEAR + i, 8 * j : 8 * j + 8, :]
+                da_ref[at] = fields_ref[k, i, 8 * j : 8 * j + 8, :]
+        for ref, up in ((ua_ref, True), (da_ref, False)):
             for dist, first in CORNER.items():
                 cols = H - dist
                 at = first % 8
                 row = CX - dist if up else dist - 1
-                ref[base + corner_entry(k, dist, 0), at : at + cols, :] = cp_ref[
+                ref[corner_entry(k, dist, 0), at : at + cols, :] = cp_ref[
                     8 * k + row, 8 - cols : 8, :
                 ]
-                ref[base + corner_entry(k, dist, 1), at : at + cols, :] = cm_ref[
-                    8 * k + row, 0:cols, :
-                ]
+                ref[corner_entry(k, dist, 1), at : at + cols, :] = cm_ref[8 * k + row, 0:cols, :]
             for side in range(2):
-                ref[base + corner_entry(k, 5, side), 7:8, :] = jnp.zeros((1, NZ), jnp.float32)
-
-
-def pack_kernel(fields_ref, ua_ref, da_ref, ub_ref, db_ref):
-    for k in range(4):
-        for i in range(NEAR):
-            ua_ref[k, i] = fields_ref[k, CX - NEAR + i]
-            da_ref[k, i] = fields_ref[k, i]
+                ref[corner_entry(k, 5, side), 7:8, :] = jnp.zeros((1, NZ), jnp.float32)
         for i in range(FAR):
             ub_ref[k, i] = fields_ref[k, CX - H + i]
             db_ref[k, i] = fields_ref[k, NEAR + i]
@@ -224,28 +224,22 @@
             dst[k, row, col : col + 8, :] = value
 
 
-def fill_sides(a, rows, e1_ref, f1_ref):
+def fill_sides(a, rows, ua_ref, da_ref):
     zero = jnp.zeros((PAD, NZ), jnp.float32)
     for k in range(4):
         for row in rows:
             a[k, row, 0:PAD, :] = zero
             a[k, row, PAD + CY :, :] = zero
-            ref, base, dist = (e1_ref, E_CORN, H - row)
-            if row >= H:
-                ref, base, dist = (f1_ref, 0, row - (H + CX - 1))
+            ref, dist = (ua_ref, H - row) if row < H else (da_ref, row - (H + CX - 1))
             if dist in CORNER:
                 cols, at = H - dist, CORNER[dist] % 8
-                a[k, row, PAD - cols : PAD, :] = ref[
-                    base + corner_entry(k, dist, 0), at : at + cols, :
+                a[k, row, PAD - cols : PAD, :] = ref[corner_entry(k, dist, 0), at : at + cols, :]
+                a[k, row, PAD + CY : PAD + CY + cols, :] = ref[
+                    corner_entry(k, dist, 1), at : at + cols, :
                 ]
-                a[k, row, PAD + CY : PAD + CY + cols, :] = ref[
-                    base + corner_entry(k, dist, 1), at : at + cols, :
-                ]
-
-
-def near_kernel(
-    flags_ref, fields_ref, ua_ref, da_ref, cp_ref, cm_ref, e1_ref, f1_ref, a, b, sem
-):
+
+
+def near_kernel(flags_ref, fields_ref, ua_ref, da_ref, cp_ref, cm_ref, a, b, sem):
     copy = pltpu.make_async_copy(fields_ref, a.at[:, H : H + CX, PAD : PAD + CY, :], sem)
     copy.start()
     edge = jnp.zeros((8, NZ), jnp.float32)
@@ -256,12 +250,14 @@
             a[k, H + row, PAD + CY : PAD + CY + 8, :] = cm_ref[8 * k + row]
             a[k, H + row, PAD + CY + 8 :, :] = edge
         for i in range(NEAR):
-            a[k, TOP + i, PAD : PAD + CY, :] = ua_ref[k, i]
-            a[k, H + CX + i, PAD : PAD + CY, :] = da_ref[k, i]
+            for j in range(8):
+                at = (k * NEAR + i) * 8 + j
+                a[k, TOP + i, PAD + 8 * j : PAD + 8 * j + 8, :] = ua_ref[at]
+                a[k, H + CX + i, PAD + 8 * j : PAD + 8 * j + 8, :] = da_ref[at]
         for row in range(TALL):
             b[k, row, 0:8, :] = edge
             b[k, row, PAD + CY + 8 :, :] = edge
-    fill_sides(a, (*range(TOP, H), *range(H + CX, H + CX + NEAR)), e1_ref, f1_ref)
+    fill_sides(a, (*range(TOP, H), *range(H + CX, H + CX + NEAR)), ua_ref, da_ref)
     copy.wait()
     ends = edges()
     for step in range(1, STEPS + 1):
@@ -274,9 +270,9 @@
 
 
 def far_kernel(
-    flags_ref, ub_ref, db_ref, e1_ref, f1_ref, deposit_ref, a_in, b_in, out_ref, a, b
+    flags_ref, ub_ref, db_ref, ua_ref, da_ref, deposit_ref, a_in, b_in, out_ref, a, b
 ):
-    fill_sides(a, (*range(FAR), *range(TALL - FAR, TALL)), e1_ref, f1_ref)
+    fill_sides(a, (*range(FAR), *range(TALL - FAR, TALL)), ua_ref, da_ref)
     for k in range(4):
         for i in range(FAR):
             a[k, i, PAD : PAD + CY, :] = ub_ref[k, i]
@@ -365,35 +361,45 @@
     )(counts, embers.reshape(21, 4, NZ), fields)
     cp = moved(cp, "cross", 1)
     cm = moved(cm, "cross", -1)
+    e1, e2 = pl.pallas_call(
+        records_kernel,
+        out_shape=(struct(6, 8, NZ), struct(6, 8, NZ)),
+        in_specs=[VMEM] * 3,
+        out_specs=(VMEM, VMEM),
+        compiler_params=PARAMS,
+        name="records",
+    )(cp, cm, own)
+    e1 = moved(e1, "down", 1)
+    e2 = moved(e2, "down", 2)
     ua, da, ub, db = pl.pallas_call(
         pack_kernel,
         out_shape=(
-            struct(4, NEAR, CY, NZ),
-            struct(4, NEAR, CY, NZ),
+            struct(A_BLOCKS, 8, NZ),
+            struct(A_BLOCKS, 8, NZ),
             struct(4, FAR, CY, NZ),
             struct(4, FAR, CY, NZ),
         ),
-        in_specs=[VMEM],
+        in_specs=[VMEM] * 3,
         out_specs=(VMEM,) * 4,
         compiler_params=PARAMS,
         name="pack",
-    )(fields)
+    )(fields, cp, cm)
     ua = moved(ua, "down", 1)
     da = moved(da, "down", -1)
-    e1, f1, e2 = pl.pallas_call(
-        records_kernel,
-        out_shape=(struct(E_CORN + 16, 8, NZ), struct(16, 8, NZ), struct(6, 8, NZ)),
-        in_specs=[VMEM] * 3,
-        out_specs=(VMEM,) * 3,
-        compiler_params=PARAMS,
-        name="records",
-    )(cp, cm, own)
-    e1 = moved(e1, "down", 1)
-    f1 = moved(f1, "down", -1)
-    e2 = moved(e2, "down", 2)
-    ub, db, e1, f1, e2 = lax.optimization_barrier((ub, db, e1, f1, e2))
     ub = moved(ub, "down", 1)
     db = moved(db, "down", -1)
+    tile = struct(4, TALL, WIDE, NZ)
+    a, b = pl.pallas_call(
+        near_kernel,
+        out_shape=(tile, tile),
+        in_specs=[SMEM, ANY, VMEM, VMEM, VMEM, VMEM],
+        out_specs=(VMEM, VMEM),
+        scratch_shapes=[pltpu.SemaphoreType.DMA],
+        compiler_params=PARAMS,
+        cost_estimate=pl.CostEstimate(flops=1_000_000_000, bytes_accessed=0, transcendentals=0),
+        name="near",
+    )(flags, fields, ua, da, cp, cm)
+    a, b, e1, e2 = lax.optimization_barrier((a, b, e1, e2))
     landed, deposit = pl.pallas_call(
         ember_kernel,
         out_shape=(struct(12, 4, NZ), struct(CX * CY, NZ)),
@@ -406,18 +412,9 @@
             pltpu.VMEM((6, 8, CAP), jnp.float32),
         ],
         compiler_params=PARAMS,
+        cost_estimate=pl.CostEstimate(flops=5_000_000_000, bytes_accessed=0, transcendentals=0),
         name="embers",
     )(fields, e1, e2)
-    tile = struct(4, TALL, WIDE, NZ)
-    a, b = pl.pallas_call(
-        near_kernel,
-        out_shape=(tile, tile),
-        in_specs=[SMEM, ANY] + [VMEM] * 6,
-        out_specs=(VMEM, VMEM),
-        scratch_shapes=[pltpu.SemaphoreType.DMA],
-        compiler_params=PARAMS,
-        name="near",
-    )(flags, fields, ua, da, cp, cm, e1, f1)
     advanced, _, _ = pl.pallas_call(
         far_kernel,
         out_shape=(struct(4, CX, CY, NZ), tile, tile),
@@ -426,7 +423,7 @@
         input_output_aliases={6: 1, 7: 2},
         compiler_params=PARAMS,
         name="far",
-    )(flags, ub, db, e1, f1, deposit.reshape(CX, CY, NZ), a, b)
+    )(flags, ub, db, ua, da, deposit.reshape(CX, CY, NZ), a, b)
     return (advanced, landed.reshape(4, 1, 1, 6, CAP))
 
 

time: 76.7 us -> 74.7 us (0.974)
  the two profiles are of different devices: /device:TPU:120 before, /device:TPU:238 now
where the time goes in v3:
time: 74.7 us; the launch traced here: 74.3 us
  starting transfers between devices  44.2 us (59%)
  Pallas kernels  22.4 us (30%)
  local copies, waits for them, and re-layouts  4.14 us (6%)
  waiting for transfers between devices  2.67 us (4%)
  between operations  0.78 us (1%)
    ppermute x8, starting transfers between devices, moved(): return lax.ppermute(x, axis, pairs)  44.2 us
    pallas_call x1, Pallas kernels, local(): pl.pallas_call(ember_kernel, out_shape=(struct(12, 4, NZ), struct(CX * CY...  8.35 us
    pallas_call x1, Pallas kernels, local(): pl.pallas_call(near_kernel, out_shape=(tile, tile), in_specs=[SMEM, ANY,...  7.4 us
    pallas_call x1, Pallas kernels, local(): pl.pallas_call(far_kernel, out_shape=(struct(4, CX, CY, NZ), tile, tile),...  5.92 us
    unnamed x10, local copies, waits for them, and re-layouts  4.14 us
    ppermute x8, waiting for transfers between devices, moved(): return lax.ppermute(x, axis, pairs)  2.67 us
  transfers between devices with their start and end apart: 8, of which 2 were waited for; matrix products, arithmetic and copies ran while one was open for 0% of the time, Pallas kernels for 21%

profile of v3, /device:TPU:238, one launch (start us, length us, event | category | flops | bytes accessed | tf_op | source)
XLA Modules:
  0.0 74.3 jit_solution(17858285374817772146)
XLA Ops:
  0.6 0.0 copy-start
  0.6 1.2 %copy-done = f32[4,8,64,128]{3,2,1,0:T(8,128)S(1)} copy-done((f32[4,8,64,128]{3,2,1,0:T(8,128)S(1)}, f32[4,8,64,128]{3,2,1,0:T(8,128)}, u32[]{:S(2)}) %copy-start) | copy-done | bytes 1048600
  1.9 0.0 copy-start.1
  1.9 0.8 %copy-done.1 = f32[7,1,1,6,256]{4,2,3,1,0:T(1,128)S(1)} copy-done((f32[7,1,1,6,256]{4,2,3,1,0:T(1,128)S(1)}, f32[7,1,1,6,256]{4,2,3,1,0:T(1,128)}, u32[]{:S(2)}) %copy-start.1) | copy-done | bytes 43032
  2.6 0.0 copy-start.2
  2.6 0.7 copy-done.2
  3.3 0.6 edges.1
  3.9 1.9 %collective-permute-start = (f32[36,8,128]{2,1,0:T(8,128)S(1)}, f32[36,8,128]{2,1,0:T(8,128)S(1)}, u32[]{:S(2)}, u32[]{:S(2)}) collective-permute-start(f32[36,8,128]{2,1,0:T(8,128)S(1)} %get-tuple-element.22), channel_id=1, source_target_pairs={{0,1},{1,2},{2,3},{4,5},{5,6},{6,7},{8,9},{9,10},{10,11},{12,13},{... | collective-permute-start | bytes 442376 | tf_op jit(solution)/shard_map/ppermute | solution.py:328
  5.9 3.6 %collective-permute-start.1 = (f32[36,8,128]{2,1,0:T(8,128)S(1)}, f32[36,8,128]{2,1,0:T(8,128)S(1)}, u32[]{:S(2)}, u32[]{:S(2)}) collective-permute-start(f32[36,8,128]{2,1,0:T(8,128)S(1)} %get-tuple-element.23), channel_id=1, source_target_pairs={{1,0},{2,1},{3,2},{5,4},{6,5},{7,6},{9,8},{10,9},{11,10},{13,12},{... | collective-permute-start | bytes 442376 | tf_op jit(solution)/shard_map/ppermute | solution.py:328
  9.5 0.9 %collective-permute-done.cp_ref = f32[36,8,128]{2,1,0:T(8,128)S(1)} collective-permute-done((f32[36,8,128]{2,1,0:T(8,128)S(1)}, f32[36,8,128]{2,1,0:T(8,128)S(1)}, u32[]{:S(2)}, u32[]{:S(2)}) %collective-permute-start) | collective-permute-done | bytes 147488 | tf_op jit(solution)/shard_map/ppermute | solution.py:328
  10.4 1.8 %collective-permute-done.1.cm_ref = f32[36,8,128]{2,1,0:T(8,128)S(1)} collective-permute-done((f32[36,8,128]{2,1,0:T(8,128)S(1)}, f32[36,8,128]{2,1,0:T(8,128)S(1)}, u32[]{:S(2)}, u32[]{:S(2)}) %collective-permute-start.1) | collective-permute-done | bytes 147488 | tf_op jit(solution)/shard_map/ppermute | solution.py:328
  12.2 0.1 pack.1
  12.3 0.0 copy-start.3
  12.3 0.7 copy-done.3
  13.0 0.0 copy-start.4
  13.0 0.7 %copy-done.4 = f32[4,3,64,128]{3,2,1,0:T(8,128)} copy-done((f32[4,3,64,128]{3,2,1,0:T(8,128)}, f32[4,3,64,128]{3,2,1,0:T(8,128)S(1)}, u32[]{:S(2)}) %copy-start.4) | copy-done | bytes 393240
  13.8 3.5 %collective-permute-start.4 = (f32[112,8,128]{2,1,0:T(8,128)S(1)}, f32[112,8,128]{2,1,0:T(8,128)S(1)}, u32[]{:S(2)}, u32[]{:S(2)}) collective-permute-start(f32[112,8,128]{2,1,0:T(8,128)S(1)} %get-tuple-element.26), channel_id=1, source_target_pairs={{0,4},{4,8},{8,12},{12,16},{16,20},{20,24},{24,28},{28,32},{32,36}... | collective-permute-start | bytes 1376264 | tf_op jit(solution)/shard_map/ppermute | solution.py:328
  17.3 2.4 %collective-permute-start.5 = (f32[112,8,128]{2,1,0:T(8,128)S(1)}, f32[112,8,128]{2,1,0:T(8,128)S(1)}, u32[]{:S(2)}, u32[]{:S(2)}) collective-permute-start(f32[112,8,128]{2,1,0:T(8,128)S(1)} %get-tuple-element.27), channel_id=1, source_target_pairs={{4,0},{8,4},{12,8},{16,12},{20,16},{24,20},{28,24},{32,28},{36,32}... | collective-permute-start | bytes 1376264 | tf_op jit(solution)/shard_map/ppermute | solution.py:328
  19.6 0.1 add_convert_fusion.flags_ref
  19.7 3.5 %collective-permute-start.6 = (f32[6,8,128]{2,1,0:T(8,128)S(1)}, f32[6,8,128]{2,1,0:T(8,128)S(1)}, u32[]{:S(2)}, u32[]{:S(2)}) collective-permute-start(f32[6,8,128]{2,1,0:T(8,128)S(1)} %get-tuple-element.31), channel_id=1, source_target_pairs={{0,4},{4,8},{8,12},{12,16},{16,20},{20,24},{24,28},{28,32},{32,36}... | collective-permute-start | bytes 73736 | tf_op jit(solution)/shard_map/ppermute | solution.py:328
  23.2 2.0 %collective-permute-start.7 = (f32[6,8,128]{2,1,0:T(8,128)S(1)}, f32[6,8,128]{2,1,0:T(8,128)S(1)}, u32[]{:S(2)}, u32[]{:S(2)}) collective-permute-start(f32[6,8,128]{2,1,0:T(8,128)S(1)} %get-tuple-element.32), channel_id=1, source_target_pairs={{0,8},{4,12},{8,16},{12,20},{16,24},{20,28},{24,32},{28,36},{32,40... | collective-permute-start | bytes 73736 | tf_op jit(solution)/shard_map/ppermute | solution.py:328
  25.3 2.5 %collective-permute-start.2 = (f32[4,3,64,128]{3,2,1,0:T(8,128)}, f32[4,3,64,128]{3,2,1,0:T(8,128)S(1)}, u32[]{:S(2)}, u32[]{:S(2)}) collective-permute-start(f32[4,3,64,128]{3,2,1,0:T(8,128)} %copy-done.4), channel_id=1, source_target_pairs={{0,4},{4,8},{8,12},{12,16},{16,20},{20,24},{24,28},{28,32},{32,36}... | collective-permute-start | bytes 1179656 | tf_op jit(solution)/shard_map/ppermute | solution.py:328
  27.8 0.0 collective-permute-done.4.ua_ref
  27.8 24.8 %collective-permute-start.3 = (f32[4,3,64,128]{3,2,1,0:T(8,128)}, f32[4,3,64,128]{3,2,1,0:T(8,128)S(1)}, u32[]{:S(2)}, u32[]{:S(2)}) collective-permute-start(f32[4,3,64,128]{3,2,1,0:T(8,128)} %copy-done.3), channel_id=1, source_target_pairs={{4,0},{8,4},{12,8},{16,12},{20,16},{24,20},{28,24},{32,28},{36,32}... | collective-permute-start | bytes 1179656 | tf_op jit(solution)/shard_map/ppermute | solution.py:328
  52.6 0.0 collective-permute-done.5.da_ref
  52.6 7.4 %near.1 = (f32[4,20,96,128]{3,2,1,0:T(8,128)S(1)}, f32[4,20,96,128]{3,2,1,0:T(8,128)S(1)}) custom-call(s32[4]{0:T(128)S(1)} %add_convert_fusion.flags_ref, f32[4,8,64,128]{3,2,1,0:T(8,128)S(1)} %get-tuple-element.21.fields_ref, f32[112,8,128]{2,1,0:T(8,128)S(1)} %collective-permute-done.4.ua_ref, f32[112,8,128]{2,1,0:T(8,128)S(1)} %collective-permute-done.5.da_ref, ...), custom_call_target="tpu_custom_call" | custom-call | flops 1000000000 | tf_op jit(solution)/shard_map/near/pallas_call | solution.py:392
  60.0 0.0 collective-permute-done.6.e1_ref
  60.0 0.0 collective-permute-done.7.e2_ref
  60.0 8.4 %embers.1 = (f32[12,4,128]{2,1,0:T(4,128)}, f32[512,128]{1,0:T(8,128)S(1)}) custom-call(f32[4,8,64,128]{3,2,1,0:T(8,128)S(1)} %get-tuple-element.21.fields_ref, f32[6,8,128]{2,1,0:T(8,128)S(1)} %collective-permute-done.6.e1_ref, f32[6,8,128]{2,1,0:T(8,128)S(1)} %collective-permute-done.7.e2_ref), custom_call_target="tpu_custom_call" | custom-call | flops 5000000000 | tf_op jit(solution)/shard_map/embers/pallas_call | solution.py:403
  68.4 0.0 collective-permute-done.2.ub_ref
  68.4 0.0 collective-permute-done.3.db_ref
  68.4 5.9 %far.1 = (f32[4,8,64,128]{3,2,1,0:T(8,128)}, f32[4,20,96,128]{3,2,1,0:T(8,128)S(1)}, f32[4,20,96,128]{3,2,1,0:T(8,128)S(1)}) custom-call(s32[4]{0:T(128)S(1)} %add_convert_fusion.flags_ref, f32[4,3,64,128]{3,2,1,0:T(8,128)S(1)} %collective-permute-done.2.ub_ref, ...), custom_call_target="tpu_custom_call", output_to_operand_aliasing={{1}: (6, {}), {2}: (7, {})} | custom-call | tf_op jit(solution)/shard_map/far/pallas_call | solution.py:418
  (1 shorter events, 0.0 us)
Async XLA Ops:
  0.6 1.2 %copy-start = (f32[4,8,64,128]{3,2,1,0:T(8,128)S(1)}, f32[4,8,64,128]{3,2,1,0:T(8,128)}, u32[]{:S(2)}) copy-start(f32[4,8,64,128]{3,2,1,0:T(8,128)} %fields_hbm.1) | copy-start | bytes 3145732
  1.9 0.8 %copy-start.1 = (f32[7,1,1,6,256]{4,2,3,1,0:T(1,128)S(1)}, f32[7,1,1,6,256]{4,2,3,1,0:T(1,128)}, u32[]{:S(2)}) copy-start(f32[7,1,1,6,256]{4,2,3,1,0:T(1,128)} %param.4) | copy-start | bytes 129028
  2.6 0.7 copy-start.2
  3.9 6.5 %collective-permute-start = (f32[36,8,128]{2,1,0:T(8,128)S(1)}, f32[36,8,128]{2,1,0:T(8,128)S(1)}, u32[]{:S(2)}, u32[]{:S(2)}) collective-permute-start(f32[36,8,128]{2,1,0:T(8,128)S(1)} %get-tuple-element.22), channel_id=1, source_target_pairs={{0,1},{1,2},{2,3},{4,5},{5,6},{6,7},{8,9},{9,10},{10,11},{12,13},{... | collective-permute-start | bytes 442376 | tf_op jit(solution)/shard_map/ppermute | solution.py:328
  5.9 6.3 %collective-permute-start.1 = (f32[36,8,128]{2,1,0:T(8,128)S(1)}, f32[36,8,128]{2,1,0:T(8,128)S(1)}, u32[]{:S(2)}, u32[]{:S(2)}) collective-permute-start(f32[36,8,128]{2,1,0:T(8,128)S(1)} %get-tuple-element.23), channel_id=1, source_target_pairs={{1,0},{2,1},{3,2},{5,4},{6,5},{7,6},{9,8},{10,9},{11,10},{13,12},{... | collective-permute-start | bytes 442376 | tf_op jit(solution)/shard_map/ppermute | solution.py:328
  12.3 0.8 %copy-start.3 = (f32[4,3,64,128]{3,2,1,0:T(8,128)}, f32[4,3,64,128]{3,2,1,0:T(8,128)S(1)}, u32[]{:S(2)}) copy-start(f32[4,3,64,128]{3,2,1,0:T(8,128)S(1)} %get-tuple-element.25) | copy-start | bytes 1179652
  13.0 0.7 %copy-start.4 = (f32[4,3,64,128]{3,2,1,0:T(8,128)}, f32[4,3,64,128]{3,2,1,0:T(8,128)S(1)}, u32[]{:S(2)}) copy-start(f32[4,3,64,128]{3,2,1,0:T(8,128)S(1)} %get-tuple-element.24) | copy-start | bytes 1179652
  13.8 14.0 %collective-permute-start.4 = (f32[112,8,128]{2,1,0:T(8,128)S(1)}, f32[112,8,128]{2,1,0:T(8,128)S(1)}, u32[]{:S(2)}, u32[]{:S(2)}) collective-permute-start(f32[112,8,128]{2,1,0:T(8,128)S(1)} %get-tuple-element.26), channel_id=1, source_target_pairs={{0,4},{4,8},{8,12},{12,16},{16,20},{20,24},{24,28},{28,32},{32,36}... | collective-permute-start | bytes 1376264 | tf_op jit(solution)/shard_map/ppermute | solution.py:328
  17.3 35.3 %collective-permute-start.5 = (f32[112,8,128]{2,1,0:T(8,128)S(1)}, f32[112,8,128]{2,1,0:T(8,128)S(1)}, u32[]{:S(2)}, u32[]{:S(2)}) collective-permute-start(f32[112,8,128]{2,1,0:T(8,128)S(1)} %get-tuple-element.27), channel_id=1, source_target_pairs={{4,0},{8,4},{12,8},{16,12},{20,16},{24,20},{28,24},{32,28},{36,32}... | collective-permute-start | bytes 1376264 | tf_op jit(solution)/shard_map/ppermute | solution.py:328
  19.7 40.3 %collective-permute-start.6 = (f32[6,8,128]{2,1,0:T(8,128)S(1)}, f32[6,8,128]{2,1,0:T(8,128)S(1)}, u32[]{:S(2)}, u32[]{:S(2)}) collective-permute-start(f32[6,8,128]{2,1,0:T(8,128)S(1)} %get-tuple-element.31), channel_id=1, source_target_pairs={{0,4},{4,8},{8,12},{12,16},{16,20},{20,24},{24,28},{28,32},{32,36}... | collective-permute-start | bytes 73736 | tf_op jit(solution)/shard_map/ppermute | solution.py:328
  23.2 36.8 %collective-permute-start.7 = (f32[6,8,128]{2,1,0:T(8,128)S(1)}, f32[6,8,128]{2,1,0:T(8,128)S(1)}, u32[]{:S(2)}, u32[]{:S(2)}) collective-permute-start(f32[6,8,128]{2,1,0:T(8,128)S(1)} %get-tuple-element.32), channel_id=1, source_target_pairs={{0,8},{4,12},{8,16},{12,20},{16,24},{20,28},{24,32},{28,36},{32,40... | collective-permute-start | bytes 73736 | tf_op jit(solution)/shard_map/ppermute | solution.py:328
  25.3 43.1 %collective-permute-start.2 = (f32[4,3,64,128]{3,2,1,0:T(8,128)}, f32[4,3,64,128]{3,2,1,0:T(8,128)S(1)}, u32[]{:S(2)}, u32[]{:S(2)}) collective-permute-start(f32[4,3,64,128]{3,2,1,0:T(8,128)} %copy-done.4), channel_id=1, source_target_pairs={{0,4},{4,8},{8,12},{12,16},{16,20},{20,24},{24,28},{28,32},{32,36}... | collective-permute-start | bytes 1179656 | tf_op jit(solution)/shard_map/ppermute | solution.py:328
  27.8 40.6 %collective-permute-start.3 = (f32[4,3,64,128]{3,2,1,0:T(8,128)}, f32[4,3,64,128]{3,2,1,0:T(8,128)S(1)}, u32[]{:S(2)}, u32[]{:S(2)}) collective-permute-start(f32[4,3,64,128]{3,2,1,0:T(8,128)} %copy-done.3), channel_id=1, source_target_pairs={{4,0},{8,4},{12,8},{16,12},{20,16},{24,20},{28,24},{32,28},{36,32}... | collective-permute-start | bytes 1179656 | tf_op jit(solution)/shard_map/ppermute | solution.py:328

commit v4 on v3

--- a/solution.py
+++ b/solution.py
@@ -83,7 +83,7 @@
         target[5, 2:8, :] = jnp.zeros((6, NZ), jnp.float32)
 
 
-def pack_kernel(fields_ref, cp_ref, cm_ref, ua_ref, da_ref, ub_ref, db_ref):
+def pack_kernel(fields_ref, cp_ref, cm_ref, ua_ref, da_ref):
     for k in range(4):
         for i in range(NEAR):
             for j in range(8):
@@ -101,6 +101,10 @@
                 ref[corner_entry(k, dist, 1), at : at + cols, :] = cm_ref[8 * k + row, 0:cols, :]
             for side in range(2):
                 ref[corner_entry(k, 5, side), 7:8, :] = jnp.zeros((1, NZ), jnp.float32)
+
+
+def far_pack_kernel(fields_ref, ub_ref, db_ref):
+    for k in range(4):
         for i in range(FAR):
             ub_ref[k, i] = fields_ref[k, CX - H + i]
             db_ref[k, i] = fields_ref[k, NEAR + i]
@@ -369,18 +373,22 @@
         compiler_params=PARAMS,
         name="records",
     )(cp, cm, own)
+    fields, e1, e2 = lax.optimization_barrier((fields, e1, e2))
+    ub, db = pl.pallas_call(
+        far_pack_kernel,
+        out_shape=(struct(4, FAR, CY, NZ), struct(4, FAR, CY, NZ)),
+        in_specs=[VMEM],
+        out_specs=(VMEM, VMEM),
+        compiler_params=PARAMS,
+        name="far_pack",
+    )(fields)
     e1 = moved(e1, "down", 1)
     e2 = moved(e2, "down", 2)
-    ua, da, ub, db = pl.pallas_call(
+    ua, da = pl.pallas_call(
         pack_kernel,
-        out_shape=(
-            struct(A_BLOCKS, 8, NZ),
-            struct(A_BLOCKS, 8, NZ),
-            struct(4, FAR, CY, NZ),
-            struct(4, FAR, CY, NZ),
-        ),
+        out_shape=(struct(A_BLOCKS, 8, NZ), struct(A_BLOCKS, 8, NZ)),
         in_specs=[VMEM] * 3,
-        out_specs=(VMEM,) * 4,
+        out_specs=(VMEM, VMEM),
         compiler_params=PARAMS,
         name="pack",
     )(fields, cp, cm)

time: 74.7 us -> 73.2 us (0.980)
  local copies, waits for them, and re-layouts: 4.14 us -> 2.66 us
    unnamed x10 -> x6, local copies, waits for them, and re-layouts: 4.14 us -> 2.66 us
  transfers between devices with their start and end apart: 8 -> 8, of which waited for: 2 -> 2; matrix products, arithmetic and copies ran while one was open for 0% -> 0% of each run, Pallas kernels for 21% -> 22%
where the time goes in v4:
time: 73.2 us; the launch traced here: 72.8 us
  starting transfers between devices  44.2 us (60%)
  Pallas kernels  22.4 us (31%)
  waiting for transfers between devices  2.67 us (4%)
  local copies, waits for them, and re-layouts  2.66 us (4%)
  between operations  0.78 us (1%)
    ppermute x8, starting transfers between devices, moved(): return lax.ppermute(x, axis, pairs)  44.2 us
    pallas_call x1, Pallas kernels, local(): pl.pallas_call(ember_kernel, out_shape=(struct(12, 4, NZ), struct(CX * CY...  8.35 us
    pallas_call x1, Pallas kernels, local(): pl.pallas_call(near_kernel, out_shape=(tile, tile), in_specs=[SMEM, ANY,...  7.4 us
    pallas_call x1, Pallas kernels, local(): pl.pallas_call(far_kernel, out_shape=(struct(4, CX, CY, NZ), tile, tile),...  5.92 us
    ppermute x8, waiting for transfers between devices, moved(): return lax.ppermute(x, axis, pairs)  2.67 us
    unnamed x6, local copies, waits for them, and re-layouts  2.66 us
  transfers between devices with their start and end apart: 8, of which 2 were waited for; matrix products, arithmetic and copies ran while one was open for 0% of the time, Pallas kernels for 22%

profile of v4, /device:TPU:238, one launch (start us, length us, event | category | flops | bytes accessed | tf_op | source)
XLA Modules:
  0.0 72.8 jit_solution(8705133643679747081)
XLA Ops:
  0.6 0.0 copy-start
  0.6 1.2 %copy-done = f32[4,8,64,128]{3,2,1,0:T(8,128)S(1)} copy-done((f32[4,8,64,128]{3,2,1,0:T(8,128)S(1)}, f32[4,8,64,128]{3,2,1,0:T(8,128)}, u32[]{:S(2)}) %copy-start) | copy-done | bytes 1048600
  1.9 0.0 copy-start.1
  1.9 0.8 %copy-done.1 = f32[7,1,1,6,256]{4,2,3,1,0:T(1,128)S(1)} copy-done((f32[7,1,1,6,256]{4,2,3,1,0:T(1,128)S(1)}, f32[7,1,1,6,256]{4,2,3,1,0:T(1,128)}, u32[]{:S(2)}) %copy-start.1) | copy-done | bytes 43032
  2.6 0.0 copy-start.2
  2.6 0.7 copy-done.2
  3.3 0.6 edges.1
  3.9 1.9 %collective-permute-start = (f32[36,8,128]{2,1,0:T(8,128)S(1)}, f32[36,8,128]{2,1,0:T(8,128)S(1)}, u32[]{:S(2)}, u32[]{:S(2)}) collective-permute-start(f32[36,8,128]{2,1,0:T(8,128)S(1)} %get-tuple-element.25), channel_id=1, source_target_pairs={{0,1},{1,2},{2,3},{4,5},{5,6},{6,7},{8,9},{9,10},{10,11},{12,13},{... | collective-permute-start | bytes 442376 | tf_op jit(solution)/shard_map/ppermute | solution.py:332
  5.9 3.6 %collective-permute-start.1 = (f32[36,8,128]{2,1,0:T(8,128)S(1)}, f32[36,8,128]{2,1,0:T(8,128)S(1)}, u32[]{:S(2)}, u32[]{:S(2)}) collective-permute-start(f32[36,8,128]{2,1,0:T(8,128)S(1)} %get-tuple-element.26), channel_id=1, source_target_pairs={{1,0},{2,1},{3,2},{5,4},{6,5},{7,6},{9,8},{10,9},{11,10},{13,12},{... | collective-permute-start | bytes 442376 | tf_op jit(solution)/shard_map/ppermute | solution.py:332
  9.5 0.9 %collective-permute-done.cp_ref = f32[36,8,128]{2,1,0:T(8,128)S(1)} collective-permute-done((f32[36,8,128]{2,1,0:T(8,128)S(1)}, f32[36,8,128]{2,1,0:T(8,128)S(1)}, u32[]{:S(2)}, u32[]{:S(2)}) %collective-permute-start) | collective-permute-done | bytes 147488 | tf_op jit(solution)/shard_map/ppermute | solution.py:332
  10.4 1.8 %collective-permute-done.1.cm_ref = f32[36,8,128]{2,1,0:T(8,128)S(1)} collective-permute-done((f32[36,8,128]{2,1,0:T(8,128)S(1)}, f32[36,8,128]{2,1,0:T(8,128)S(1)}, u32[]{:S(2)}, u32[]{:S(2)}) %collective-permute-start.1) | collective-permute-done | bytes 147488 | tf_op jit(solution)/shard_map/ppermute | solution.py:332
  12.2 0.1 pack.1
  12.3 3.5 %collective-permute-start.4 = (f32[112,8,128]{2,1,0:T(8,128)S(1)}, f32[112,8,128]{2,1,0:T(8,128)S(1)}, u32[]{:S(2)}, u32[]{:S(2)}) collective-permute-start(f32[112,8,128]{2,1,0:T(8,128)S(1)} %get-tuple-element.33), channel_id=1, source_target_pairs={{0,4},{4,8},{8,12},{12,16},{16,20},{20,24},{24,28},{28,32},{32,36}... | collective-permute-start | bytes 1376264 | tf_op jit(solution)/shard_map/ppermute | solution.py:332
  15.8 2.4 %collective-permute-start.5 = (f32[112,8,128]{2,1,0:T(8,128)S(1)}, f32[112,8,128]{2,1,0:T(8,128)S(1)}, u32[]{:S(2)}, u32[]{:S(2)}) collective-permute-start(f32[112,8,128]{2,1,0:T(8,128)S(1)} %get-tuple-element.34), channel_id=1, source_target_pairs={{4,0},{8,4},{12,8},{16,12},{20,16},{24,20},{28,24},{32,28},{36,32}... | collective-permute-start | bytes 1376264 | tf_op jit(solution)/shard_map/ppermute | solution.py:332
  18.1 0.1 add_convert_fusion.flags_ref
  18.2 0.1 far_pack.1
  18.3 3.5 %collective-permute-start.6 = (f32[6,8,128]{2,1,0:T(8,128)S(1)}, f32[6,8,128]{2,1,0:T(8,128)S(1)}, u32[]{:S(2)}, u32[]{:S(2)}) collective-permute-start(f32[6,8,128]{2,1,0:T(8,128)S(1)} %get-tuple-element.37), channel_id=1, source_target_pairs={{0,4},{4,8},{8,12},{12,16},{16,20},{20,24},{24,28},{28,32},{32,36}... | collective-permute-start | bytes 73736 | tf_op jit(solution)/shard_map/ppermute | solution.py:332
  21.8 2.0 %collective-permute-start.7 = (f32[6,8,128]{2,1,0:T(8,128)S(1)}, f32[6,8,128]{2,1,0:T(8,128)S(1)}, u32[]{:S(2)}, u32[]{:S(2)}) collective-permute-start(f32[6,8,128]{2,1,0:T(8,128)S(1)} %get-tuple-element.38), channel_id=1, source_target_pairs={{0,8},{4,12},{8,16},{12,20},{16,24},{20,28},{24,32},{28,36},{32,40... | collective-permute-start | bytes 73736 | tf_op jit(solution)/shard_map/ppermute | solution.py:332
  23.8 2.5 %collective-permute-start.2 = (f32[4,3,64,128]{3,2,1,0:T(8,128)S(1)}, f32[4,3,64,128]{3,2,1,0:T(8,128)S(1)}, u32[]{:S(2)}, u32[]{:S(2)}) collective-permute-start(f32[4,3,64,128]{3,2,1,0:T(8,128)S(1)} %get-tuple-element.31), channel_id=1, source_target_pairs={{0,4},{4,8},{8,12},{12,16},{16,20},{20,24},{24,28},{28,32},{32,36}... | collective-permute-start | bytes 1179656 | tf_op jit(solution)/shard_map/ppermute | solution.py:332
  26.3 0.0 collective-permute-done.4.ua_ref
  26.3 24.8 %collective-permute-start.3 = (f32[4,3,64,128]{3,2,1,0:T(8,128)S(1)}, f32[4,3,64,128]{3,2,1,0:T(8,128)S(1)}, u32[]{:S(2)}, u32[]{:S(2)}) collective-permute-start(f32[4,3,64,128]{3,2,1,0:T(8,128)S(1)} %get-tuple-element.32), channel_id=1, source_target_pairs={{4,0},{8,4},{12,8},{16,12},{20,16},{24,20},{28,24},{32,28},{36,32}... | collective-permute-start | bytes 1179656 | tf_op jit(solution)/shard_map/ppermute | solution.py:332
  51.1 0.0 collective-permute-done.5.da_ref
  51.1 7.4 %near.1 = (f32[4,20,96,128]{3,2,1,0:T(8,128)S(1)}, f32[4,20,96,128]{3,2,1,0:T(8,128)S(1)}) custom-call(s32[4]{0:T(128)S(1)} %add_convert_fusion.flags_ref, f32[4,8,64,128]{3,2,1,0:T(8,128)S(1)} %get-tuple-element.30.fields_ref, f32[112,8,128]{2,1,0:T(8,128)S(1)} %collective-permute-done.4.ua_ref, f32[112,8,128]{2,1,0:T(8,128)S(1)} %collective-permute-done.5.da_ref, ...), custom_call_target="tpu_custom_call" | custom-call | flops 1000000000 | tf_op jit(solution)/shard_map/near/pallas_call | solution.py:400
  58.5 0.0 collective-permute-done.6.e1_ref
  58.5 0.0 collective-permute-done.7.e2_ref
  58.5 8.4 %embers.1 = (f32[12,4,128]{2,1,0:T(4,128)}, f32[512,128]{1,0:T(8,128)S(1)}) custom-call(f32[4,8,64,128]{3,2,1,0:T(8,128)S(1)} %get-tuple-element.30.fields_ref, f32[6,8,128]{2,1,0:T(8,128)S(1)} %collective-permute-done.6.e1_ref, f32[6,8,128]{2,1,0:T(8,128)S(1)} %collective-permute-done.7.e2_ref), custom_call_target="tpu_custom_call" | custom-call | flops 5000000000 | tf_op jit(solution)/shard_map/embers/pallas_call | solution.py:411
  66.9 0.0 collective-permute-done.2.ub_ref
  66.9 0.0 collective-permute-done.3.db_ref
  66.9 5.9 %far.1 = (f32[4,8,64,128]{3,2,1,0:T(8,128)}, f32[4,20,96,128]{3,2,1,0:T(8,128)S(1)}, f32[4,20,96,128]{3,2,1,0:T(8,128)S(1)}) custom-call(s32[4]{0:T(128)S(1)} %add_convert_fusion.flags_ref, f32[4,3,64,128]{3,2,1,0:T(8,128)S(1)} %collective-permute-done.2.ub_ref, ...), custom_call_target="tpu_custom_call", output_to_operand_aliasing={{1}: (6, {}), {2}: (7, {})} | custom-call | tf_op jit(solution)/shard_map/far/pallas_call | solution.py:426
  (1 shorter events, 0.0 us)
Async XLA Ops:
  0.6 1.2 %copy-start = (f32[4,8,64,128]{3,2,1,0:T(8,128)S(1)}, f32[4,8,64,128]{3,2,1,0:T(8,128)}, u32[]{:S(2)}) copy-start(f32[4,8,64,128]{3,2,1,0:T(8,128)} %fields_hbm.1) | copy-start | bytes 3145732
  1.9 0.8 %copy-start.1 = (f32[7,1,1,6,256]{4,2,3,1,0:T(1,128)S(1)}, f32[7,1,1,6,256]{4,2,3,1,0:T(1,128)}, u32[]{:S(2)}) copy-start(f32[7,1,1,6,256]{4,2,3,1,0:T(1,128)} %param.4) | copy-start | bytes 129028
  2.6 0.7 copy-start.2
  3.9 6.5 %collective-permute-start = (f32[36,8,128]{2,1,0:T(8,128)S(1)}, f32[36,8,128]{2,1,0:T(8,128)S(1)}, u32[]{:S(2)}, u32[]{:S(2)}) collective-permute-start(f32[36,8,128]{2,1,0:T(8,128)S(1)} %get-tuple-element.25), channel_id=1, source_target_pairs={{0,1},{1,2},{2,3},{4,5},{5,6},{6,7},{8,9},{9,10},{10,11},{12,13},{... | collective-permute-start | bytes 442376 | tf_op jit(solution)/shard_map/ppermute | solution.py:332
  5.9 6.3 %collective-permute-start.1 = (f32[36,8,128]{2,1,0:T(8,128)S(1)}, f32[36,8,128]{2,1,0:T(8,128)S(1)}, u32[]{:S(2)}, u32[]{:S(2)}) collective-permute-start(f32[36,8,128]{2,1,0:T(8,128)S(1)} %get-tuple-element.26), channel_id=1, source_target_pairs={{1,0},{2,1},{3,2},{5,4},{6,5},{7,6},{9,8},{10,9},{11,10},{13,12},{... | collective-permute-start | bytes 442376 | tf_op jit(solution)/shard_map/ppermute | solution.py:332
  12.3 14.0 %collective-permute-start.4 = (f32[112,8,128]{2,1,0:T(8,128)S(1)}, f32[112,8,128]{2,1,0:T(8,128)S(1)}, u32[]{:S(2)}, u32[]{:S(2)}) collective-permute-start(f32[112,8,128]{2,1,0:T(8,128)S(1)} %get-tuple-element.33), channel_id=1, source_target_pairs={{0,4},{4,8},{8,12},{12,16},{16,20},{20,24},{24,28},{28,32},{32,36}... | collective-permute-start | bytes 1376264 | tf_op jit(solution)/shard_map/ppermute | solution.py:332
  15.8 35.3 %collective-permute-start.5 = (f32[112,8,128]{2,1,0:T(8,128)S(1)}, f32[112,8,128]{2,1,0:T(8,128)S(1)}, u32[]{:S(2)}, u32[]{:S(2)}) collective-permute-start(f32[112,8,128]{2,1,0:T(8,128)S(1)} %get-tuple-element.34), channel_id=1, source_target_pairs={{4,0},{8,4},{12,8},{16,12},{20,16},{24,20},{28,24},{32,28},{36,32}... | collective-permute-start | bytes 1376264 | tf_op jit(solution)/shard_map/ppermute | solution.py:332
  18.3 40.2 %collective-permute-start.6 = (f32[6,8,128]{2,1,0:T(8,128)S(1)}, f32[6,8,128]{2,1,0:T(8,128)S(1)}, u32[]{:S(2)}, u32[]{:S(2)}) collective-permute-start(f32[6,8,128]{2,1,0:T(8,128)S(1)} %get-tuple-element.37), channel_id=1, source_target_pairs={{0,4},{4,8},{8,12},{12,16},{16,20},{20,24},{24,28},{28,32},{32,36}... | collective-permute-start | bytes 73736 | tf_op jit(solution)/shard_map/ppermute | solution.py:332
  21.8 36.8 %collective-permute-start.7 = (f32[6,8,128]{2,1,0:T(8,128)S(1)}, f32[6,8,128]{2,1,0:T(8,128)S(1)}, u32[]{:S(2)}, u32[]{:S(2)}) collective-permute-start(f32[6,8,128]{2,1,0:T(8,128)S(1)} %get-tuple-element.38), channel_id=1, source_target_pairs={{0,8},{4,12},{8,16},{12,20},{16,24},{20,28},{24,32},{28,36},{32,40... | collective-permute-start | bytes 73736 | tf_op jit(solution)/shard_map/ppermute | solution.py:332
  23.8 43.1 %collective-permute-start.2 = (f32[4,3,64,128]{3,2,1,0:T(8,128)S(1)}, f32[4,3,64,128]{3,2,1,0:T(8,128)S(1)}, u32[]{:S(2)}, u32[]{:S(2)}) collective-permute-start(f32[4,3,64,128]{3,2,1,0:T(8,128)S(1)} %get-tuple-element.31), channel_id=1, source_target_pairs={{0,4},{4,8},{8,12},{12,16},{16,20},{20,24},{24,28},{28,32},{32,36}... | collective-permute-start | bytes 1179656 | tf_op jit(solution)/shard_map/ppermute | solution.py:332
  26.3 40.6 %collective-permute-start.3 = (f32[4,3,64,128]{3,2,1,0:T(8,128)S(1)}, f32[4,3,64,128]{3,2,1,0:T(8,128)S(1)}, u32[]{:S(2)}, u32[]{:S(2)}) collective-permute-start(f32[4,3,64,128]{3,2,1,0:T(8,128)S(1)} %get-tuple-element.32), channel_id=1, source_target_pairs={{4,0},{8,4},{12,8},{16,12},{20,16},{24,20},{28,24},{32,28},{36,32}... | collective-permute-start | bytes 1179656 | tf_op jit(solution)/shard_map/ppermute | solution.py:332

commit v5 on v4

--- a/solution.py
+++ b/solution.py
@@ -16,7 +16,7 @@
 CX, CY, NZ = 8, 64, 128
 CAP = 256
 H = STEPS
-NEAR = 3
+NEAR = 2
 FAR = H - NEAR
 PAD = 16
 WIDE = CY + 2 * PAD

time: 73.2 us -> 71.7 us (0.980)
  the two profiles are of different devices: /device:TPU:238 before, /device:TPU:89 now
where the time goes in v5:
time: 71.7 us; the launch traced here: 71.3 us
  starting transfers between devices  27.6 us (38%)
  Pallas kernels  22.3 us (31%)
  waiting for transfers between devices  17.9 us (25%)
  local copies, waits for them, and re-layouts  2.66 us (4%)
  between operations  0.77 us (1%)
    ppermute x8, starting transfers between devices, moved(): return lax.ppermute(x, axis, pairs)  27.6 us
    ppermute x8, waiting for transfers between devices, moved(): return lax.ppermute(x, axis, pairs)  17.9 us
    pallas_call x1, Pallas kernels, local(): pl.pallas_call(ember_kernel, out_shape=(struct(12, 4, NZ), struct(CX * CY...  8.35 us
    pallas_call x1, Pallas kernels, local(): pl.pallas_call(far_kernel, out_shape=(struct(4, CX, CY, NZ), tile, tile),...  7.65 us
    pallas_call x1, Pallas kernels, local(): pl.pallas_call(near_kernel, out_shape=(tile, tile), in_specs=[SMEM, ANY,...  5.49 us
    unnamed x6, local copies, waits for them, and re-layouts  2.66 us
  transfers between devices with their start and end apart: 8, of which 3 were waited for; matrix products, arithmetic and copies ran while one was open for 0% of the time, Pallas kernels for 20%

profile of v5, /device:TPU:89, one launch (start us, length us, event | category | flops | bytes accessed | tf_op | source)
XLA Modules:
  0.0 71.3 jit_solution(1528847433205506852)
XLA Ops:
  0.6 0.0 copy-start
  0.6 1.2 %copy-done = f32[4,8,64,128]{3,2,1,0:T(8,128)S(1)} copy-done((f32[4,8,64,128]{3,2,1,0:T(8,128)S(1)}, f32[4,8,64,128]{3,2,1,0:T(8,128)}, u32[]{:S(2)}) %copy-start) | copy-done | bytes 1048600
  1.9 0.0 copy-start.1
  1.9 0.8 %copy-done.1 = f32[7,1,1,6,256]{4,2,3,1,0:T(1,128)S(1)} copy-done((f32[7,1,1,6,256]{4,2,3,1,0:T(1,128)S(1)}, f32[7,1,1,6,256]{4,2,3,1,0:T(1,128)}, u32[]{:S(2)}) %copy-start.1) | copy-done | bytes 43032
  2.6 0.0 copy-start.2
  2.6 0.7 copy-done.2
  3.3 0.6 edges.1
  3.9 4.1 %collective-permute-start = (f32[36,8,128]{2,1,0:T(8,128)S(1)}, f32[36,8,128]{2,1,0:T(8,128)S(1)}, u32[]{:S(2)}, u32[]{:S(2)}) collective-permute-start(f32[36,8,128]{2,1,0:T(8,128)S(1)} %get-tuple-element.25), channel_id=1, source_target_pairs={{0,1},{1,2},{2,3},{4,5},{5,6},{6,7},{8,9},{9,10},{10,11},{12,13},{... | collective-permute-start | bytes 442376 | tf_op jit(solution)/shard_map/ppermute | solution.py:332
  8.0 1.9 %collective-permute-start.1 = (f32[36,8,128]{2,1,0:T(8,128)S(1)}, f32[36,8,128]{2,1,0:T(8,128)S(1)}, u32[]{:S(2)}, u32[]{:S(2)}) collective-permute-start(f32[36,8,128]{2,1,0:T(8,128)S(1)} %get-tuple-element.26), channel_id=1, source_target_pairs={{1,0},{2,1},{3,2},{5,4},{6,5},{7,6},{9,8},{10,9},{11,10},{13,12},{... | collective-permute-start | bytes 442376 | tf_op jit(solution)/shard_map/ppermute | solution.py:332
  10.0 0.2 collective-permute-done.cp_ref
  10.1 4.4 %collective-permute-done.1.cm_ref = f32[36,8,128]{2,1,0:T(8,128)S(1)} collective-permute-done((f32[36,8,128]{2,1,0:T(8,128)S(1)}, f32[36,8,128]{2,1,0:T(8,128)S(1)}, u32[]{:S(2)}, u32[]{:S(2)}) %collective-permute-start.1) | collective-permute-done | bytes 147488 | tf_op jit(solution)/shard_map/ppermute | solution.py:332
  14.5 0.1 pack.1
  14.6 4.9 %collective-permute-start.4 = (f32[80,8,128]{2,1,0:T(8,128)S(1)}, f32[80,8,128]{2,1,0:T(8,128)S(1)}, u32[]{:S(2)}, u32[]{:S(2)}) collective-permute-start(f32[80,8,128]{2,1,0:T(8,128)S(1)} %get-tuple-element.33), channel_id=1, source_target_pairs={{0,4},{4,8},{8,12},{12,16},{16,20},{20,24},{24,28},{28,32},{32,36}... | collective-permute-start | bytes 983048 | tf_op jit(solution)/shard_map/ppermute | solution.py:332
  19.5 1.9 %collective-permute-start.5 = (f32[80,8,128]{2,1,0:T(8,128)S(1)}, f32[80,8,128]{2,1,0:T(8,128)S(1)}, u32[]{:S(2)}, u32[]{:S(2)}) collective-permute-start(f32[80,8,128]{2,1,0:T(8,128)S(1)} %get-tuple-element.34), channel_id=1, source_target_pairs={{4,0},{8,4},{12,8},{16,12},{20,16},{24,20},{28,24},{32,28},{36,32}... | collective-permute-start | bytes 983048 | tf_op jit(solution)/shard_map/ppermute | solution.py:332
  21.4 0.1 add_convert_fusion.flags_ref
  21.5 0.1 far_pack.1
  21.6 7.6 %collective-permute-start.6 = (f32[6,8,128]{2,1,0:T(8,128)S(1)}, f32[6,8,128]{2,1,0:T(8,128)S(1)}, u32[]{:S(2)}, u32[]{:S(2)}) collective-permute-start(f32[6,8,128]{2,1,0:T(8,128)S(1)} %get-tuple-element.37), channel_id=1, source_target_pairs={{0,4},{4,8},{8,12},{12,16},{16,20},{20,24},{24,28},{28,32},{32,36}... | collective-permute-start | bytes 73736 | tf_op jit(solution)/shard_map/ppermute | solution.py:332
  29.1 1.9 %collective-permute-start.7 = (f32[6,8,128]{2,1,0:T(8,128)S(1)}, f32[6,8,128]{2,1,0:T(8,128)S(1)}, u32[]{:S(2)}, u32[]{:S(2)}) collective-permute-start(f32[6,8,128]{2,1,0:T(8,128)S(1)} %get-tuple-element.38), channel_id=1, source_target_pairs={{0,8},{4,12},{8,16},{12,20},{16,24},{20,28},{24,32},{28,36},{32,40... | collective-permute-start | bytes 73736 | tf_op jit(solution)/shard_map/ppermute | solution.py:332
  31.1 1.9 %collective-permute-start.2 = (f32[4,4,64,128]{3,2,1,0:T(8,128)S(1)}, f32[4,4,64,128]{3,2,1,0:T(8,128)S(1)}, u32[]{:S(2)}, u32[]{:S(2)}) collective-permute-start(f32[4,4,64,128]{3,2,1,0:T(8,128)S(1)} %get-tuple-element.31), channel_id=1, source_target_pairs={{0,4},{4,8},{8,12},{12,16},{16,20},{20,24},{24,28},{28,32},{32,36}... | collective-permute-start | bytes 1572872 | tf_op jit(solution)/shard_map/ppermute | solution.py:332
  33.0 0.0 collective-permute-done.4.ua_ref
  33.0 3.4 %collective-permute-start.3 = (f32[4,4,64,128]{3,2,1,0:T(8,128)S(1)}, f32[4,4,64,128]{3,2,1,0:T(8,128)S(1)}, u32[]{:S(2)}, u32[]{:S(2)}) collective-permute-start(f32[4,4,64,128]{3,2,1,0:T(8,128)S(1)} %get-tuple-element.32), channel_id=1, source_target_pairs={{4,0},{8,4},{12,8},{16,12},{20,16},{24,20},{28,24},{32,28},{36,32}... | collective-permute-start | bytes 1572872 | tf_op jit(solution)/shard_map/ppermute | solution.py:332
  36.4 13.4 %collective-permute-done.5.da_ref = f32[80,8,128]{2,1,0:T(8,128)S(1)} collective-permute-done((f32[80,8,128]{2,1,0:T(8,128)S(1)}, f32[80,8,128]{2,1,0:T(8,128)S(1)}, u32[]{:S(2)}, u32[]{:S(2)}) %collective-permute-start.5) | collective-permute-done | bytes 327712 | tf_op jit(solution)/shard_map/ppermute | solution.py:332
  49.8 5.5 %near.1 = (f32[4,20,96,128]{3,2,1,0:T(8,128)S(1)}, f32[4,20,96,128]{3,2,1,0:T(8,128)S(1)}) custom-call(s32[4]{0:T(128)S(1)} %add_convert_fusion.flags_ref, f32[4,8,64,128]{3,2,1,0:T(8,128)S(1)} %get-tuple-element.30.fields_ref, f32[80,8,128]{2,1,0:T(8,128)S(1)} %collective-permute-done.4.ua_ref, f32[80,8,128]{2,1,0:T(8,128)S(1)} %collective-permute-done.5.da_ref, ...), custom_call_target="tpu_custom_call" | custom-call | flops 1000000000 | tf_op jit(solution)/shard_map/near/pallas_call | solution.py:400
  55.3 0.0 collective-permute-done.6.e1_ref
  55.3 0.0 collective-permute-done.7.e2_ref
  55.3 8.4 %embers.1 = (f32[12,4,128]{2,1,0:T(4,128)}, f32[512,128]{1,0:T(8,128)S(1)}) custom-call(f32[4,8,64,128]{3,2,1,0:T(8,128)S(1)} %get-tuple-element.30.fields_ref, f32[6,8,128]{2,1,0:T(8,128)S(1)} %collective-permute-done.6.e1_ref, f32[6,8,128]{2,1,0:T(8,128)S(1)} %collective-permute-done.7.e2_ref), custom_call_target="tpu_custom_call" | custom-call | flops 5000000000 | tf_op jit(solution)/shard_map/embers/pallas_call | solution.py:411
  63.7 0.0 collective-permute-done.2.ub_ref
  63.7 0.0 collective-permute-done.3.db_ref
  63.7 7.6 %far.1 = (f32[4,8,64,128]{3,2,1,0:T(8,128)}, f32[4,20,96,128]{3,2,1,0:T(8,128)S(1)}, f32[4,20,96,128]{3,2,1,0:T(8,128)S(1)}) custom-call(s32[4]{0:T(128)S(1)} %add_convert_fusion.flags_ref, f32[4,4,64,128]{3,2,1,0:T(8,128)S(1)} %collective-permute-done.2.ub_ref, ...), custom_call_target="tpu_custom_call", output_to_operand_aliasing={{1}: (6, {}), {2}: (7, {})} | custom-call | tf_op jit(solution)/shard_map/far/pallas_call | solution.py:426
  (1 shorter events, 0.0 us)
Async XLA Ops:
  0.6 1.2 %copy-start = (f32[4,8,64,128]{3,2,1,0:T(8,128)S(1)}, f32[4,8,64,128]{3,2,1,0:T(8,128)}, u32[]{:S(2)}) copy-start(f32[4,8,64,128]{3,2,1,0:T(8,128)} %fields_hbm.1) | copy-start | bytes 3145732
  1.9 0.8 %copy-start.1 = (f32[7,1,1,6,256]{4,2,3,1,0:T(1,128)S(1)}, f32[7,1,1,6,256]{4,2,3,1,0:T(1,128)}, u32[]{:S(2)}) copy-start(f32[7,1,1,6,256]{4,2,3,1,0:T(1,128)} %param.4) | copy-start | bytes 129028
  2.6 0.7 copy-start.2
  3.9 6.2 %collective-permute-start = (f32[36,8,128]{2,1,0:T(8,128)S(1)}, f32[36,8,128]{2,1,0:T(8,128)S(1)}, u32[]{:S(2)}, u32[]{:S(2)}) collective-permute-start(f32[36,8,128]{2,1,0:T(8,128)S(1)} %get-tuple-element.25), channel_id=1, source_target_pairs={{0,1},{1,2},{2,3},{4,5},{5,6},{6,7},{8,9},{9,10},{10,11},{12,13},{... | collective-permute-start | bytes 442376 | tf_op jit(solution)/shard_map/ppermute | solution.py:332
  8.0 6.5 %collective-permute-start.1 = (f32[36,8,128]{2,1,0:T(8,128)S(1)}, f32[36,8,128]{2,1,0:T(8,128)S(1)}, u32[]{:S(2)}, u32[]{:S(2)}) collective-permute-start(f32[36,8,128]{2,1,0:T(8,128)S(1)} %get-tuple-element.26), channel_id=1, source_target_pairs={{1,0},{2,1},{3,2},{5,4},{6,5},{7,6},{9,8},{10,9},{11,10},{13,12},{... | collective-permute-start | bytes 442376 | tf_op jit(solution)/shard_map/ppermute | solution.py:332
  14.6 18.4 %collective-permute-start.4 = (f32[80,8,128]{2,1,0:T(8,128)S(1)}, f32[80,8,128]{2,1,0:T(8,128)S(1)}, u32[]{:S(2)}, u32[]{:S(2)}) collective-permute-start(f32[80,8,128]{2,1,0:T(8,128)S(1)} %get-tuple-element.33), channel_id=1, source_target_pairs={{0,4},{4,8},{8,12},{12,16},{16,20},{20,24},{24,28},{28,32},{32,36}... | collective-permute-start | bytes 983048 | tf_op jit(solution)/shard_map/ppermute | solution.py:332
  19.5 30.3 %collective-permute-start.5 = (f32[80,8,128]{2,1,0:T(8,128)S(1)}, f32[80,8,128]{2,1,0:T(8,128)S(1)}, u32[]{:S(2)}, u32[]{:S(2)}) collective-permute-start(f32[80,8,128]{2,1,0:T(8,128)S(1)} %get-tuple-element.34), channel_id=1, source_target_pairs={{4,0},{8,4},{12,8},{16,12},{20,16},{24,20},{28,24},{32,28},{36,32}... | collective-permute-start | bytes 983048 | tf_op jit(solution)/shard_map/ppermute | solution.py:332
  21.6 33.7 %collective-permute-start.6 = (f32[6,8,128]{2,1,0:T(8,128)S(1)}, f32[6,8,128]{2,1,0:T(8,128)S(1)}, u32[]{:S(2)}, u32[]{:S(2)}) collective-permute-start(f32[6,8,128]{2,1,0:T(8,128)S(1)} %get-tuple-element.37), channel_id=1, source_target_pairs={{0,4},{4,8},{8,12},{12,16},{16,20},{20,24},{24,28},{28,32},{32,36}... | collective-permute-start | bytes 73736 | tf_op jit(solution)/shard_map/ppermute | solution.py:332
  29.1 26.1 %collective-permute-start.7 = (f32[6,8,128]{2,1,0:T(8,128)S(1)}, f32[6,8,128]{2,1,0:T(8,128)S(1)}, u32[]{:S(2)}, u32[]{:S(2)}) collective-permute-start(f32[6,8,128]{2,1,0:T(8,128)S(1)} %get-tuple-element.38), channel_id=1, source_target_pairs={{0,8},{4,12},{8,16},{12,20},{16,24},{20,28},{24,32},{28,36},{32,40... | collective-permute-start | bytes 73736 | tf_op jit(solution)/shard_map/ppermute | solution.py:332
  31.1 32.6 %collective-permute-start.2 = (f32[4,4,64,128]{3,2,1,0:T(8,128)S(1)}, f32[4,4,64,128]{3,2,1,0:T(8,128)S(1)}, u32[]{:S(2)}, u32[]{:S(2)}) collective-permute-start(f32[4,4,64,128]{3,2,1,0:T(8,128)S(1)} %get-tuple-element.31), channel_id=1, source_target_pairs={{0,4},{4,8},{8,12},{12,16},{16,20},{20,24},{24,28},{28,32},{32,36}... | collective-permute-start | bytes 1572872 | tf_op jit(solution)/shard_map/ppermute | solution.py:332
  33.0 30.6 %collective-permute-start.3 = (f32[4,4,64,128]{3,2,1,0:T(8,128)S(1)}, f32[4,4,64,128]{3,2,1,0:T(8,128)S(1)}, u32[]{:S(2)}, u32[]{:S(2)}) collective-permute-start(f32[4,4,64,128]{3,2,1,0:T(8,128)S(1)} %get-tuple-element.32), channel_id=1, source_target_pairs={{4,0},{8,4},{12,8},{16,12},{20,16},{24,20},{28,24},{32,28},{36,32}... | collective-permute-start | bytes 1572872 | tf_op jit(solution)/shard_map/ppermute | solution.py:332

commit v6 on v5

--- a/solution.py
+++ b/solution.py
@@ -16,7 +16,7 @@
 CX, CY, NZ = 8, 64, 128
 CAP = 256
 H = STEPS
-NEAR = 2
+NEAR = 1
 FAR = H - NEAR
 PAD = 16
 WIDE = CY + 2 * PAD
@@ -420,7 +420,7 @@
             pltpu.VMEM((6, 8, CAP), jnp.float32),
         ],
         compiler_params=PARAMS,
-        cost_estimate=pl.CostEstimate(flops=5_000_000_000, bytes_accessed=0, transcendentals=0),
+        cost_estimate=pl.CostEstimate(flops=8_000_000_000, bytes_accessed=0, transcendentals=0),
         name="embers",
     )(fields, e1, e2)
     advanced, _, _ = pl.pallas_call(

time: 71.7 us -> 75.7 us (1.056)
  the two profiles are of different devices: /device:TPU:89 before, /device:TPU:7 now
where the time goes in v6:
time: 75.7 us; the launch traced here: 74.6 us
  starting transfers between devices  31.9 us (42%)
  Pallas kernels  21.9 us (29%)
  waiting for transfers between devices  17.2 us (23%)
  local copies, waits for them, and re-layouts  2.66 us (4%)
  between operations  0.78 us (1%)
    ppermute x8, starting transfers between devices, moved(): return lax.ppermute(x, axis, pairs)  31.9 us
    ppermute x8, waiting for transfers between devices, moved(): return lax.ppermute(x, axis, pairs)  17.2 us
    pallas_call x1, Pallas kernels, local(): pl.pallas_call(far_kernel, out_shape=(struct(4, CX, CY, NZ), tile, tile),...  8.89 us
    pallas_call x1, Pallas kernels, local(): pl.pallas_call(ember_kernel, out_shape=(struct(12, 4, NZ), struct(CX * CY...  8.35 us
    pallas_call x1, Pallas kernels, local(): pl.pallas_call(near_kernel, out_shape=(tile, tile), in_specs=[SMEM, ANY,...  3.89 us
    unnamed x6, local copies, waits for them, and re-layouts  2.66 us
  transfers between devices with their start and end apart: 8, of which 4 were waited for; matrix products, arithmetic and copies ran while one was open for 0% of the time, Pallas kernels for 17%

profile of v6, /device:TPU:7, one launch (start us, length us, event | category | flops | bytes accessed | tf_op | source)
XLA Modules:
  0.0 74.6 jit_solution(14646632018017604078)
XLA Ops:
  0.6 0.0 copy-start
  0.6 1.2 %copy-done = f32[4,8,64,128]{3,2,1,0:T(8,128)S(1)} copy-done((f32[4,8,64,128]{3,2,1,0:T(8,128)S(1)}, f32[4,8,64,128]{3,2,1,0:T(8,128)}, u32[]{:S(2)}) %copy-start) | copy-done | bytes 1048600
  1.9 0.0 copy-start.1
  1.9 0.8 %copy-done.1 = f32[7,1,1,6,256]{4,2,3,1,0:T(1,128)S(1)} copy-done((f32[7,1,1,6,256]{4,2,3,1,0:T(1,128)S(1)}, f32[7,1,1,6,256]{4,2,3,1,0:T(1,128)}, u32[]{:S(2)}) %copy-start.1) | copy-done | bytes 43032
  2.6 0.0 copy-start.2
  2.6 0.7 copy-done.2
  3.3 0.6 edges.1
  3.9 4.1 %collective-permute-start = (f32[36,8,128]{2,1,0:T(8,128)S(1)}, f32[36,8,128]{2,1,0:T(8,128)S(1)}, u32[]{:S(2)}, u32[]{:S(2)}) collective-permute-start(f32[36,8,128]{2,1,0:T(8,128)S(1)} %get-tuple-element.25), channel_id=1, source_target_pairs={{0,1},{1,2},{2,3},{4,5},{5,6},{6,7},{8,9},{9,10},{10,11},{12,13},{... | collective-permute-start | bytes 442376 | tf_op jit(solution)/shard_map/ppermute | solution.py:332
  8.0 1.9 %collective-permute-start.1 = (f32[36,8,128]{2,1,0:T(8,128)S(1)}, f32[36,8,128]{2,1,0:T(8,128)S(1)}, u32[]{:S(2)}, u32[]{:S(2)}) collective-permute-start(f32[36,8,128]{2,1,0:T(8,128)S(1)} %get-tuple-element.26), channel_id=1, source_target_pairs={{1,0},{2,1},{3,2},{5,4},{6,5},{7,6},{9,8},{10,9},{11,10},{13,12},{... | collective-permute-start | bytes 442376 | tf_op jit(solution)/shard_map/ppermute | solution.py:332
  10.0 0.2 collective-permute-done.cp_ref
  10.1 4.4 %collective-permute-done.1.cm_ref = f32[36,8,128]{2,1,0:T(8,128)S(1)} collective-permute-done((f32[36,8,128]{2,1,0:T(8,128)S(1)}, f32[36,8,128]{2,1,0:T(8,128)S(1)}, u32[]{:S(2)}, u32[]{:S(2)}) %collective-permute-start.1) | collective-permute-done | bytes 147488 | tf_op jit(solution)/shard_map/ppermute | solution.py:332
  14.6 3.2 %collective-permute-start.4 = (f32[48,8,128]{2,1,0:T(8,128)S(1)}, f32[48,8,128]{2,1,0:T(8,128)S(1)}, u32[]{:S(2)}, u32[]{:S(2)}) collective-permute-start(f32[48,8,128]{2,1,0:T(8,128)S(1)} %get-tuple-element.33), channel_id=1, source_target_pairs={{0,4},{4,8},{8,12},{12,16},{16,20},{20,24},{24,28},{28,32},{32,36}... | collective-permute-start | bytes 589832 | tf_op jit(solution)/shard_map/ppermute | solution.py:332
  17.8 8.5 %collective-permute-start.5 = (f32[48,8,128]{2,1,0:T(8,128)S(1)}, f32[48,8,128]{2,1,0:T(8,128)S(1)}, u32[]{:S(2)}, u32[]{:S(2)}) collective-permute-start(f32[48,8,128]{2,1,0:T(8,128)S(1)} %get-tuple-element.34), channel_id=1, source_target_pairs={{4,0},{8,4},{12,8},{16,12},{20,16},{24,20},{28,24},{32,28},{36,32}... | collective-permute-start | bytes 589832 | tf_op jit(solution)/shard_map/ppermute | solution.py:332
  26.3 0.1 add_convert_fusion.flags_ref
  26.3 0.1 far_pack.1
  26.4 1.9 %collective-permute-start.6 = (f32[6,8,128]{2,1,0:T(8,128)S(1)}, f32[6,8,128]{2,1,0:T(8,128)S(1)}, u32[]{:S(2)}, u32[]{:S(2)}) collective-permute-start(f32[6,8,128]{2,1,0:T(8,128)S(1)} %get-tuple-element.37), channel_id=1, source_target_pairs={{0,4},{4,8},{8,12},{12,16},{16,20},{20,24},{24,28},{28,32},{32,36}... | collective-permute-start | bytes 73736 | tf_op jit(solution)/shard_map/ppermute | solution.py:332
  28.4 1.9 %collective-permute-start.7 = (f32[6,8,128]{2,1,0:T(8,128)S(1)}, f32[6,8,128]{2,1,0:T(8,128)S(1)}, u32[]{:S(2)}, u32[]{:S(2)}) collective-permute-start(f32[6,8,128]{2,1,0:T(8,128)S(1)} %get-tuple-element.38), channel_id=1, source_target_pairs={{0,8},{4,12},{8,16},{12,20},{16,24},{20,28},{24,32},{28,36},{32,40... | collective-permute-start | bytes 73736 | tf_op jit(solution)/shard_map/ppermute | solution.py:332
  30.3 4.5 %collective-permute-start.2 = (f32[4,5,64,128]{3,2,1,0:T(8,128)S(1)}, f32[4,5,64,128]{3,2,1,0:T(8,128)S(1)}, u32[]{:S(2)}, u32[]{:S(2)}) collective-permute-start(f32[4,5,64,128]{3,2,1,0:T(8,128)S(1)} %get-tuple-element.31), channel_id=1, source_target_pairs={{0,4},{4,8},{8,12},{12,16},{16,20},{20,24},{24,28},{28,32},{32,36}... | collective-permute-start | bytes 1966088 | tf_op jit(solution)/shard_map/ppermute | solution.py:332
  34.8 0.0 collective-permute-done.4.ua_ref
  34.8 5.9 %collective-permute-start.3 = (f32[4,5,64,128]{3,2,1,0:T(8,128)S(1)}, f32[4,5,64,128]{3,2,1,0:T(8,128)S(1)}, u32[]{:S(2)}, u32[]{:S(2)}) collective-permute-start(f32[4,5,64,128]{3,2,1,0:T(8,128)S(1)} %get-tuple-element.32), channel_id=1, source_target_pairs={{4,0},{8,4},{12,8},{16,12},{20,16},{24,20},{28,24},{32,28},{36,32}... | collective-permute-start | bytes 1966088 | tf_op jit(solution)/shard_map/ppermute | solution.py:332
  40.7 0.0 collective-permute-done.5.da_ref
  40.7 3.9 %near.1 = (f32[4,20,96,128]{3,2,1,0:T(8,128)S(1)}, f32[4,20,96,128]{3,2,1,0:T(8,128)S(1)}) custom-call(s32[4]{0:T(128)S(1)} %add_convert_fusion.flags_ref, f32[4,8,64,128]{3,2,1,0:T(8,128)S(1)} %get-tuple-element.30.fields_ref, f32[48,8,128]{2,1,0:T(8,128)S(1)} %collective-permute-done.4.ua_ref, f32[48,8,128]{2,1,0:T(8,128)S(1)} %collective-permute-done.5.da_ref, ...), custom_call_target="tpu_custom_call" | custom-call | flops 1000000000 | tf_op jit(solution)/shard_map/near/pallas_call | solution.py:400
  44.6 0.0 collective-permute-done.6.e1_ref
  44.6 0.0 collective-permute-done.7.e2_ref
  44.7 8.4 %embers.1 = (f32[12,4,128]{2,1,0:T(4,128)}, f32[512,128]{1,0:T(8,128)S(1)}) custom-call(f32[4,8,64,128]{3,2,1,0:T(8,128)S(1)} %get-tuple-element.30.fields_ref, f32[6,8,128]{2,1,0:T(8,128)S(1)} %collective-permute-done.6.e1_ref, f32[6,8,128]{2,1,0:T(8,128)S(1)} %collective-permute-done.7.e2_ref), custom_call_target="tpu_custom_call" | custom-call | flops 8000000000 | tf_op jit(solution)/shard_map/embers/pallas_call | solution.py:411
  53.0 11.9 %collective-permute-done.2.ub_ref = f32[4,5,64,128]{3,2,1,0:T(8,128)S(1)} collective-permute-done((f32[4,5,64,128]{3,2,1,0:T(8,128)S(1)}, f32[4,5,64,128]{3,2,1,0:T(8,128)S(1)}, u32[]{:S(2)}, u32[]{:S(2)}) %collective-permute-start.2) | collective-permute-done | bytes 655392 | tf_op jit(solution)/shard_map/ppermute | solution.py:332
  64.9 0.8 %collective-permute-done.3.db_ref = f32[4,5,64,128]{3,2,1,0:T(8,128)S(1)} collective-permute-done((f32[4,5,64,128]{3,2,1,0:T(8,128)S(1)}, f32[4,5,64,128]{3,2,1,0:T(8,128)S(1)}, u32[]{:S(2)}, u32[]{:S(2)}) %collective-permute-start.3) | collective-permute-done | bytes 655392 | tf_op jit(solution)/shard_map/ppermute | solution.py:332
  65.7 8.9 %far.1 = (f32[4,8,64,128]{3,2,1,0:T(8,128)}, f32[4,20,96,128]{3,2,1,0:T(8,128)S(1)}, f32[4,20,96,128]{3,2,1,0:T(8,128)S(1)}) custom-call(s32[4]{0:T(128)S(1)} %add_convert_fusion.flags_ref, f32[4,5,64,128]{3,2,1,0:T(8,128)S(1)} %collective-permute-done.2.ub_ref, ...), custom_call_target="tpu_custom_call", output_to_operand_aliasing={{1}: (6, {}), {2}: (7, {})} | custom-call | tf_op jit(solution)/shard_map/far/pallas_call | solution.py:426
  (2 shorter events, 0.1 us)
Async XLA Ops:
  0.6 1.2 %copy-start = (f32[4,8,64,128]{3,2,1,0:T(8,128)S(1)}, f32[4,8,64,128]{3,2,1,0:T(8,128)}, u32[]{:S(2)}) copy-start(f32[4,8,64,128]{3,2,1,0:T(8,128)} %fields_hbm.1) | copy-start | bytes 3145732
  1.9 0.8 %copy-start.1 = (f32[7,1,1,6,256]{4,2,3,1,0:T(1,128)S(1)}, f32[7,1,1,6,256]{4,2,3,1,0:T(1,128)}, u32[]{:S(2)}) copy-start(f32[7,1,1,6,256]{4,2,3,1,0:T(1,128)} %param.4) | copy-start | bytes 129028
  2.6 0.7 copy-start.2
  3.9 6.2 %collective-permute-start = (f32[36,8,128]{2,1,0:T(8,128)S(1)}, f32[36,8,128]{2,1,0:T(8,128)S(1)}, u32[]{:S(2)}, u32[]{:S(2)}) collective-permute-start(f32[36,8,128]{2,1,0:T(8,128)S(1)} %get-tuple-element.25), channel_id=1, source_target_pairs={{0,1},{1,2},{2,3},{4,5},{5,6},{6,7},{8,9},{9,10},{10,11},{12,13},{... | collective-permute-start | bytes 442376 | tf_op jit(solution)/shard_map/ppermute | solution.py:332
  8.0 6.5 %collective-permute-start.1 = (f32[36,8,128]{2,1,0:T(8,128)S(1)}, f32[36,8,128]{2,1,0:T(8,128)S(1)}, u32[]{:S(2)}, u32[]{:S(2)}) collective-permute-start(f32[36,8,128]{2,1,0:T(8,128)S(1)} %get-tuple-element.26), channel_id=1, source_target_pairs={{1,0},{2,1},{3,2},{5,4},{6,5},{7,6},{9,8},{10,9},{11,10},{13,12},{... | collective-permute-start | bytes 442376 | tf_op jit(solution)/shard_map/ppermute | solution.py:332
  14.6 20.2 %collective-permute-start.4 = (f32[48,8,128]{2,1,0:T(8,128)S(1)}, f32[48,8,128]{2,1,0:T(8,128)S(1)}, u32[]{:S(2)}, u32[]{:S(2)}) collective-permute-start(f32[48,8,128]{2,1,0:T(8,128)S(1)} %get-tuple-element.33), channel_id=1, source_target_pairs={{0,4},{4,8},{8,12},{12,16},{16,20},{20,24},{24,28},{28,32},{32,36}... | collective-permute-start | bytes 589832 | tf_op jit(solution)/shard_map/ppermute | solution.py:332
  17.8 22.9 %collective-permute-start.5 = (f32[48,8,128]{2,1,0:T(8,128)S(1)}, f32[48,8,128]{2,1,0:T(8,128)S(1)}, u32[]{:S(2)}, u32[]{:S(2)}) collective-permute-start(f32[48,8,128]{2,1,0:T(8,128)S(1)} %get-tuple-element.34), channel_id=1, source_target_pairs={{4,0},{8,4},{12,8},{16,12},{20,16},{24,20},{28,24},{32,28},{36,32}... | collective-permute-start | bytes 589832 | tf_op jit(solution)/shard_map/ppermute | solution.py:332
  26.4 18.2 %collective-permute-start.6 = (f32[6,8,128]{2,1,0:T(8,128)S(1)}, f32[6,8,128]{2,1,0:T(8,128)S(1)}, u32[]{:S(2)}, u32[]{:S(2)}) collective-permute-start(f32[6,8,128]{2,1,0:T(8,128)S(1)} %get-tuple-element.37), channel_id=1, source_target_pairs={{0,4},{4,8},{8,12},{12,16},{16,20},{20,24},{24,28},{28,32},{32,36}... | collective-permute-start | bytes 73736 | tf_op jit(solution)/shard_map/ppermute | solution.py:332
  28.4 16.3 %collective-permute-start.7 = (f32[6,8,128]{2,1,0:T(8,128)S(1)}, f32[6,8,128]{2,1,0:T(8,128)S(1)}, u32[]{:S(2)}, u32[]{:S(2)}) collective-permute-start(f32[6,8,128]{2,1,0:T(8,128)S(1)} %get-tuple-element.38), channel_id=1, source_target_pairs={{0,8},{4,12},{8,16},{12,20},{16,24},{20,28},{24,32},{28,36},{32,40... | collective-permute-start | bytes 73736 | tf_op jit(solution)/shard_map/ppermute | solution.py:332
  30.3 34.6 %collective-permute-start.2 = (f32[4,5,64,128]{3,2,1,0:T(8,128)S(1)}, f32[4,5,64,128]{3,2,1,0:T(8,128)S(1)}, u32[]{:S(2)}, u32[]{:S(2)}) collective-permute-start(f32[4,5,64,128]{3,2,1,0:T(8,128)S(1)} %get-tuple-element.31), channel_id=1, source_target_pairs={{0,4},{4,8},{8,12},{12,16},{16,20},{20,24},{24,28},{28,32},{32,36}... | collective-permute-start | bytes 1966088 | tf_op jit(solution)/shard_map/ppermute | solution.py:332
  34.8 30.9 %collective-permute-start.3 = (f32[4,5,64,128]{3,2,1,0:T(8,128)S(1)}, f32[4,5,64,128]{3,2,1,0:T(8,128)S(1)}, u32[]{:S(2)}, u32[]{:S(2)}) collective-permute-start(f32[4,5,64,128]{3,2,1,0:T(8,128)S(1)} %get-tuple-element.32), channel_id=1, source_target_pairs={{4,0},{8,4},{12,8},{16,12},{20,16},{24,20},{28,24},{32,28},{36,32}... | collective-permute-start | bytes 1966088 | tf_op jit(solution)/shard_map/ppermute | solution.py:332
